TPU v7x, 32 devices: a whole 2x2x4 slice. The times are simulated.
32 devices in a mesh: dp: 16 (over z, y, core), tensor: 2 (over x).
Axes of the slice: x: 2, y: 2, z: 4, core: 2. Of those that a mesh axis runs over, the one named last changes fastest.
Arguments:
- tokens: bfloat16 [16384, 1024], P(('dp', 'tensor')), may hold values from -6 to 6
- lengths: int32 [16, 4], P('dp'), may hold values from 0 to 1024, as said below
- attn_gain: bfloat16 [1024], P('dp'), may hold values from 0.5 to 1.5
- w_query: bfloat16 [1024, 1024], P('dp', 'tensor'), may hold values from -0.1875 to 0.1875
- key_weight: bfloat16 [1024, 512], P('dp', 'tensor'), may hold values from -0.1875 to 0.1875
- value_weight: bfloat16 [1024, 512], P('dp', 'tensor'), may hold values from -0.1875 to 0.1875
- query_gain: bfloat16 [64], replicated, may hold values from 0.5 to 1.5
- key_gain: bfloat16 [64], replicated, may hold values from 0.5 to 1.5
- w_out: bfloat16 [1024, 1024], P('tensor', 'dp'), may hold values from -3 to 3
- ffn_gain: bfloat16 [1024], P('dp'), may hold values from 0.5 to 1.5
- w_gate: bfloat16 [1024, 4608], P('dp', 'tensor'), may hold values from -0.1875 to 0.1875
- w_up: bfloat16 [1024, 4608], P('dp', 'tensor'), may hold values from -0.1875 to 0.1875
- w_down: bfloat16 [4608, 1024], P('tensor', 'dp'), may hold values from -0.09375 to 0.09375
- out_grad: bfloat16 [16384, 1024], P(('dp', 'tensor')), may hold values from -6 to 6
Outputs:
- output: bfloat16 [16384, 1024], P(('dp', 'tensor'))
- input_grad: float32 [16384, 1024], P(('dp', 'tensor'))
- attn_gain_grad: float32 [1024], P('dp')
- w_query_grad: float32 [1024, 1024], P('dp', 'tensor')
- w_key_grad: float32 [1024, 512], P('dp', 'tensor')
- w_value_grad: float32 [1024, 512], P('dp', 'tensor')
- query_gain_grad: float32 [64], replicated
- key_gain_grad: float32 [64], replicated
- w_out_grad: float32 [1024, 1024], P('tensor', 'dp')
- ffn_gain_grad: float32 [1024], P('dp')
- w_gate_grad: float32 [1024, 4608], P('dp', 'tensor')
- w_up_grad: float32 [1024, 4608], P('dp', 'tensor')
- w_down_grad: float32 [4608, 1024], P('tensor', 'dp')
Inputs may be any that keep to these rules, and one draw needn't show every extreme that they name: Each row lists the lengths of one group's sequences in slot order, packed from the group's first slot; a row sums to at most 1024 and the slots after the last sequence are padding.
All inputs are finite; a program needn't handle non-finite values.
Results may differ from a plain program's by a relative error of at most 0.018.
Values may be sent and summed in bfloat16 or wider, within the bound.
A program may use at most 256 MiB of HBM per device.

v0:
```python
import jax
import jax.numpy as jnp
from jax import lax
from jax.sharding import PartitionSpec as P

EPSILON = 1e-05
ROPE_BASE = 1000000.0
MASK_FILL = -1e30


def segments(seq_lengths, total_slots):
    ends = jnp.cumsum(seq_lengths)
    starts = ends - seq_lengths
    places = jnp.arange(total_slots, dtype=jnp.int32)
    segment_index = jnp.sum((places[:, None] >= ends[None, :]).astype(jnp.int32), axis=1)
    number = seq_lengths.shape[0]
    chosen = segment_index[:, None] == jnp.arange(number, dtype=jnp.int32)[None, :]
    first_slot = jnp.sum(jnp.where(chosen, starts[None, :], 0), axis=1)
    return (segment_index, places - first_slot, segment_index < number)


def block_mask(segment_index, valid_mask, low_row, high_row, key_count):
    query_places = jnp.arange(low_row, high_row)
    key_places = jnp.arange(key_count)
    causal = key_places[None, :] <= query_places[:, None]
    same = (
        (segment_index[low_row:high_row, None] == segment_index[None, :key_count])
        & valid_mask[low_row:high_row, None]
        & causal
    )
    return same | (key_places[None, :] == query_places[:, None])


def rows_normalize(values, gain_vec):
    inverse = lax.rsqrt(jnp.mean(values * values, axis=-1, keepdims=True) + EPSILON)
    return (values * inverse * gain_vec, inverse)


def norm_back(values, inverse, gain_vec, grad_in):
    scaled = grad_in * gain_vec
    inner_mean = jnp.mean(scaled * values, axis=-1, keepdims=True)
    return (
        inverse * (scaled - values * inverse * inverse * inner_mean),
        grad_in * values * inverse,
    )


def rope_tables(position, width):
    half_width = width // 2
    frequency = ROPE_BASE ** (-(jnp.arange(half_width).astype(jnp.float32) * 2.0 / width))
    angles = position.astype(jnp.float32)[:, None] * frequency[None, :]
    return (jnp.cos(angles)[:, None, :], jnp.sin(angles)[:, None, :])


def apply_rotary(values, cosine_table, sine_table):
    half_width = values.shape[-1] // 2
    first_half = values[..., :half_width]
    second_half = values[..., half_width:]
    return jnp.concatenate(
        [
            first_half * cosine_table - second_half * sine_table,
            second_half * cosine_table + first_half * sine_table,
        ],
        axis=-1,
    )


def unrotate(grad_in, cosine_table, sine_table):
    half_width = grad_in.shape[-1] // 2
    first_half = grad_in[..., :half_width]
    second_half = grad_in[..., half_width:]
    return jnp.concatenate(
        [
            first_half * cosine_table + second_half * sine_table,
            second_half * cosine_table - first_half * sine_table,
        ],
        axis=-1,
    )


def contract_rows(left, right):
    return lax.dot_general(
        left, right, (((0,), (0,)), ((), ())), preferred_element_type=jnp.float32
    )


def contract_cols(left, right):
    return lax.dot_general(
        left, right, (((1,), (1,)), ((), ())), preferred_element_type=jnp.float32
    )


def per_device(
    tokens,
    lengths,
    attn_gain,
    w_query,
    key_weight,
    value_weight,
    query_gain,
    key_gain,
    w_out,
    ffn_gain,
    w_gate,
    w_up,
    w_down,
    out_grad,
):
    tok_rows = tokens.shape[0]
    group_rows = tok_rows * lax.axis_size("tensor")
    head_dim = query_gain.shape[0]
    kv_heads = key_weight.shape[1] // head_dim
    query_heads = w_query.shape[1] // head_dim
    repeat = query_heads // kv_heads
    blk_rows = min(512, group_rows)
    score_scale = head_dim ** (-0.5)
    segment_index, position, valid_mask = segments(lengths[0], group_rows)
    first_row = lax.axis_index("tensor") * tok_rows
    valid_local = lax.dynamic_slice_in_dim(valid_mask, first_row, tok_rows, 0)
    cosine_table, sine_table = rope_tables(position, head_dim)
    qgain_wide = query_gain.astype(jnp.float32)
    kgain_wide = key_gain.astype(jnp.float32)
    wq_all, wk_all, wv_all, wo_all, attn_gain_all = (
        lax.all_gather(w_query, "dp", axis=0, tiled=True),
        lax.all_gather(key_weight, "dp", axis=0, tiled=True),
        lax.all_gather(value_weight, "dp", axis=0, tiled=True),
        lax.all_gather(w_out, "dp", axis=1, tiled=True),
        lax.all_gather(attn_gain, "dp", axis=0, tiled=True),
    )
    tokens_wide = tokens.astype(jnp.float32)
    attn_in, attn_inv = rows_normalize(tokens_wide, attn_gain_all.astype(jnp.float32))
    attn_rows = lax.all_gather(attn_in.astype(jnp.bfloat16), "tensor", axis=0, tiled=True)
    query_raw = jnp.dot(attn_rows, wq_all, preferred_element_type=jnp.float32).reshape(
        group_rows, query_heads, head_dim
    )
    key_unrotated = jnp.dot(attn_rows, wk_all, preferred_element_type=jnp.float32).reshape(
        group_rows, kv_heads, head_dim
    )
    value_lowered = (
        jnp.dot(attn_rows, wv_all, preferred_element_type=jnp.float32)
        .astype(jnp.bfloat16)
        .reshape(group_rows, kv_heads, head_dim)
    )
    query_normed, query_inv = rows_normalize(query_raw, qgain_wide)
    key_normed, key_inv = rows_normalize(key_unrotated, kgain_wide)
    query_low = apply_rotary(query_normed, cosine_table, sine_table).astype(jnp.bfloat16)
    key_low = apply_rotary(key_normed, cosine_table, sine_table).astype(jnp.bfloat16)
    query_grouped = query_low.reshape(group_rows, kv_heads, repeat, head_dim)
    outputs = []
    kept_stats = []
    for number in range(group_rows // blk_rows):
        low_row = number * blk_rows
        high_row = low_row + blk_rows
        allowed = block_mask(segment_index, valid_mask, low_row, high_row, high_row)
        scores = (
            jnp.einsum(
                "qgrd,kgd->grqk",
                query_grouped[low_row:high_row],
                key_low[:high_row],
                preferred_element_type=jnp.float32,
            )
            * score_scale
        )
        scores = jnp.where(allowed[None, None], scores, MASK_FILL)
        row_peak = jnp.max(scores, axis=-1, keepdims=True)
        exp_terms = jnp.exp(scores - row_peak)
        row_total = jnp.sum(exp_terms, axis=-1, keepdims=True)
        probs_low = (exp_terms / row_total).astype(jnp.bfloat16)
        outputs.append(
            jnp.einsum(
                "grqk,kgd->qgrd",
                probs_low,
                value_lowered[:high_row],
                preferred_element_type=jnp.float32,
            )
        )
        kept_stats.append((row_peak, row_total))
    heads_low = (
        jnp.concatenate(outputs, axis=0)
        .reshape(group_rows, query_heads * head_dim)
        .astype(jnp.bfloat16)
    )
    mixed = tokens_wide + lax.psum_scatter(
        jnp.dot(heads_low, wo_all, preferred_element_type=jnp.float32),
        "tensor",
        scatter_dimension=0,
        tiled=True,
    )
    wg_all, wu_all, wd_all, ffn_gain_all = (
        lax.all_gather(w_gate, "dp", axis=0, tiled=True),
        lax.all_gather(w_up, "dp", axis=0, tiled=True),
        lax.all_gather(w_down, "dp", axis=1, tiled=True),
        lax.all_gather(ffn_gain, "dp", axis=0, tiled=True),
    )
    ffn_in, ffn_inv = rows_normalize(mixed, ffn_gain_all.astype(jnp.float32))
    ffn_rows = lax.all_gather(ffn_in.astype(jnp.bfloat16), "tensor", axis=0, tiled=True)
    gate = jnp.dot(ffn_rows, wg_all, preferred_element_type=jnp.float32)
    up_proj = jnp.dot(ffn_rows, wu_all, preferred_element_type=jnp.float32)
    hidden = (jax.nn.silu(gate) * up_proj).astype(jnp.bfloat16)
    result = mixed + lax.psum_scatter(
        jnp.dot(hidden, wd_all, preferred_element_type=jnp.float32).astype(jnp.bfloat16),
        "tensor",
        scatter_dimension=0,
        tiled=True,
    ).astype(jnp.float32)
    output = result.astype(jnp.bfloat16)
    wq_all, wk_all, wv_all, wo_all, attn_gain_all, wg_all, wu_all, wd_all, ffn_gain_all = (
        lax.all_gather(w_query, "dp", axis=0, tiled=True),
        lax.all_gather(key_weight, "dp", axis=0, tiled=True),
        lax.all_gather(value_weight, "dp", axis=0, tiled=True),
        lax.all_gather(w_out, "dp", axis=1, tiled=True),
        lax.all_gather(attn_gain, "dp", axis=0, tiled=True),
        lax.all_gather(w_gate, "dp", axis=0, tiled=True),
        lax.all_gather(w_up, "dp", axis=0, tiled=True),
        lax.all_gather(w_down, "dp", axis=1, tiled=True),
        lax.all_gather(ffn_gain, "dp", axis=0, tiled=True),
    )
    grad_out = jnp.where(valid_local[:, None], out_grad, jnp.zeros_like(out_grad))
    grad_rows = lax.all_gather(grad_out, "tensor", axis=0, tiled=True)
    grad_hidden = contract_cols(grad_rows, wd_all)
    grad_down = contract_rows(hidden, grad_rows)
    sigmoid_gate = jax.nn.sigmoid(gate)
    grad_up_low = (grad_hidden * gate * sigmoid_gate).astype(jnp.bfloat16)
    grad_gate_low = (
        grad_hidden * up_proj * sigmoid_gate * (1.0 + gate * (1.0 - sigmoid_gate))
    ).astype(jnp.bfloat16)
    grad_gate_w = contract_rows(ffn_rows, grad_gate_low)
    grad_up_w = contract_rows(ffn_rows, grad_up_low)
    gate_part = contract_cols(grad_gate_low, wg_all)
    grad_ffn_in = lax.psum_scatter(
        (gate_part + contract_cols(grad_up_low, wu_all)).astype(jnp.bfloat16),
        "tensor",
        scatter_dimension=0,
        tiled=True,
    ).astype(jnp.float32)
    back_mixed, ffn_gain_part = norm_back(
        mixed, ffn_inv, ffn_gain_all.astype(jnp.float32), grad_ffn_in
    )
    grad_mixed = grad_out.astype(jnp.float32) + back_mixed
    ffn_sums = (
        lax.psum_scatter(
            grad_gate_w.astype(jnp.bfloat16), "dp", scatter_dimension=0, tiled=True
        ).astype(jnp.float32),
        lax.psum_scatter(
            grad_up_w.astype(jnp.bfloat16), "dp", scatter_dimension=0, tiled=True
        ).astype(jnp.float32),
        lax.psum_scatter(
            grad_down.astype(jnp.bfloat16), "dp", scatter_dimension=1, tiled=True
        ).astype(jnp.float32),
    )
    grad_mixed_rows = lax.all_gather(grad_mixed.astype(jnp.bfloat16), "tensor", axis=0, tiled=True)
    grad_heads = (
        contract_cols(grad_mixed_rows, wo_all)
        .astype(jnp.bfloat16)
        .reshape(group_rows, kv_heads, repeat, head_dim)
    )
    grad_wo = contract_rows(heads_low, grad_mixed_rows)
    grad_query_parts = []
    grad_key = jnp.zeros((group_rows, kv_heads, head_dim), jnp.float32)
    grad_value = jnp.zeros((group_rows, kv_heads, head_dim), jnp.float32)
    for number in range(group_rows // blk_rows):
        low_row = number * blk_rows
        high_row = low_row + blk_rows
        row_peak, row_total = kept_stats[number]
        allowed = block_mask(segment_index, valid_mask, low_row, high_row, high_row)
        scores = (
            jnp.einsum(
                "qgrd,kgd->grqk",
                query_grouped[low_row:high_row],
                key_low[:high_row],
                preferred_element_type=jnp.float32,
            )
            * score_scale
        )
        scores = jnp.where(allowed[None, None], scores, MASK_FILL)
        probs_wide = jnp.exp(scores - row_peak) / row_total
        probs_low = probs_wide.astype(jnp.bfloat16)
        grad_probs = jnp.einsum(
            "qgrd,kgd->grqk",
            grad_heads[low_row:high_row],
            value_lowered[:high_row],
            preferred_element_type=jnp.float32,
        )
        inner_sum = jnp.sum(probs_wide * grad_probs, axis=-1, keepdims=True)
        grad_scores = (probs_wide * (grad_probs - inner_sum)).astype(jnp.bfloat16)
        grad_query_parts.append(
            jnp.einsum(
                "grqk,kgd->qgrd",
                grad_scores,
                key_low[:high_row],
                preferred_element_type=jnp.float32,
            )
            * score_scale
        )
        grad_key = grad_key.at[:high_row].add(
            jnp.einsum(
                "grqk,qgrd->kgd",
                grad_scores,
                query_grouped[low_row:high_row],
                preferred_element_type=jnp.float32,
            )
            * score_scale
        )
        grad_value = grad_value.at[:high_row].add(
            jnp.einsum(
                "grqk,qgrd->kgd",
                probs_low,
                grad_heads[low_row:high_row],
                preferred_element_type=jnp.float32,
            )
        )
    grad_query_all = jnp.concatenate(grad_query_parts, axis=0).reshape(
        group_rows, query_heads, head_dim
    )
    grad_query_raw, qgain_terms = norm_back(
        query_raw, query_inv, qgain_wide, unrotate(grad_query_all, cosine_table, sine_table)
    )
    grad_key_raw, kgain_terms = norm_back(
        key_unrotated, key_inv, kgain_wide, unrotate(grad_key, cosine_table, sine_table)
    )
    grad_query_low = grad_query_raw.reshape(group_rows, query_heads * head_dim).astype(jnp.bfloat16)
    grad_key_low = grad_key_raw.reshape(group_rows, kv_heads * head_dim).astype(jnp.bfloat16)
    grad_value_low = grad_value.reshape(group_rows, kv_heads * head_dim).astype(jnp.bfloat16)
    grad_wq = contract_rows(attn_rows, grad_query_low)
    grad_wk = contract_rows(attn_rows, grad_key_low)
    grad_wv = contract_rows(attn_rows, grad_value_low)
    query_part = contract_cols(grad_query_low, wq_all)
    key_part = contract_cols(grad_key_low, wk_all)
    value_part = contract_cols(grad_value_low, wv_all)
    grad_attn_in = lax.psum_scatter(
        (query_part + key_part + value_part).astype(jnp.bfloat16),
        "tensor",
        scatter_dimension=0,
        tiled=True,
    ).astype(jnp.float32)
    back_tokens, attn_gain_part = norm_back(
        tokens_wide, attn_inv, attn_gain_all.astype(jnp.float32), grad_attn_in
    )
    input_grad = grad_mixed + back_tokens
    attn_sums = (
        lax.psum_scatter(
            grad_wq.astype(jnp.bfloat16), "dp", scatter_dimension=0, tiled=True
        ).astype(jnp.float32),
        lax.psum_scatter(
            grad_wk.astype(jnp.bfloat16), "dp", scatter_dimension=0, tiled=True
        ).astype(jnp.float32),
        lax.psum_scatter(
            grad_wv.astype(jnp.bfloat16), "dp", scatter_dimension=0, tiled=True
        ).astype(jnp.float32),
        lax.psum_scatter(
            grad_wo.astype(jnp.bfloat16), "dp", scatter_dimension=1, tiled=True
        ).astype(jnp.float32),
    )
    gain_sums = lax.psum(
        (
            jnp.sum(attn_gain_part, axis=0),
            jnp.sum(ffn_gain_part, axis=0),
            jnp.sum(qgain_terms, axis=(0, 1)),
            jnp.sum(kgain_terms, axis=(0, 1)),
        ),
        ("dp", "tensor"),
    )
    gain_shard = attn_gain.shape[0]
    gain_start = lax.axis_index("dp") * gain_shard
    attn_gain_grad = lax.dynamic_slice_in_dim(gain_sums[0], gain_start, gain_shard, 0)
    ffn_gain_grad = lax.dynamic_slice_in_dim(gain_sums[1], gain_start, gain_shard, 0)
    return (
        output,
        input_grad,
        attn_gain_grad,
        attn_sums[0],
        attn_sums[1],
        attn_sums[2],
        gain_sums[2],
        gain_sums[3],
        attn_sums[3],
        ffn_gain_grad,
        ffn_sums[0],
        ffn_sums[1],
        ffn_sums[2],
    )


def solution(mesh):
    in_specs = (
        P(("dp", "tensor"), None),
        P("dp", None),
        P("dp"),
        P("dp", "tensor"),
        P("dp", "tensor"),
        P("dp", "tensor"),
        P(),
        P(),
        P("tensor", "dp"),
        P("dp"),
        P("dp", "tensor"),
        P("dp", "tensor"),
        P("tensor", "dp"),
        P(("dp", "tensor"), None),
    )
    out_specs = (
        P(("dp", "tensor"), None),
        P(("dp", "tensor"), None),
        P("dp"),
        P("dp", "tensor"),
        P("dp", "tensor"),
        P("dp", "tensor"),
        P(),
        P(),
        P("tensor", "dp"),
        P("dp"),
        P("dp", "tensor"),
        P("dp", "tensor"),
        P("tensor", "dp"),
    )
    return jax.shard_map(
        per_device, mesh=mesh, in_specs=in_specs, out_specs=out_specs, check_vma=False
    )
```

profile of v0, /device:TPU:0, one launch (start us, length us, event | category | flops | bytes accessed | tf_op | source)
XLA Modules:
  0.0 1120.1 jit_solution(12816110785233293351)
XLA Ops:
  12.4 34.9 %all-reduce.5 = (bf16[1024]{0:T(1024)(128)(2,1)S(1)}, bf16[1024]{0:T(1024)(128)(2,1)S(1)}) all-reduce(bf16[1024]{0:T(1024)(128)(2,1)S(1)} %dynamic-update-slice.10, bf16[1024]{0:T(1024)(128)(2,1)S(1)} %dynamic-update-slice.11), channel_id=1, replica_groups=mesh['dp'=16,'tensor'=2] {'dp'}, use_global_device_ids=true, to_apply=%add.2 | all-reduce | flops 2048 | bytes 8192
  52.5 18.7 %all_gather.51 = bf16[1024,256]{1,0:T(8,128)(2,1)S(1)} all-gather(bf16[64,256]{1,0:T(8,128)(2,1)S(1)} %copy-done.51), channel_id=1, replica_groups=mesh['dp'=16,'tensor'=2] {'dp'}, dimensions={0}, use_global_device_ids=true | all-gather | bytes 557056 | tf_op jit(solution)/shard_map/all_gather | solution.py:125
  71.2 21.0 %all_gather.50 = bf16[1024,256]{1,0:T(8,128)(2,1)S(1)} all-gather(bf16[64,256]{1,0:T(8,128)(2,1)S(1)} %copy-done.52), channel_id=1, replica_groups=mesh['dp'=16,'tensor'=2] {'dp'}, dimensions={0}, use_global_device_ids=true | all-gather | bytes 557056 | tf_op jit(solution)/shard_map/all_gather | solution.py:126
  97.4 23.8 %all-gather.12.cloned.1.call-done = bf16[1024,512]{1,0:T(8,128)(2,1)} async-done(((bf16[64,512]{1,0:T(8,128)(2,1)}), bf16[1024,512]{1,0:T(8,128)(2,1)}) %all-gather.12.cloned.1.call-update) | async-done | bytes 1048592 | tf_op jit(solution)/shard_map/all_gather | solution.py:124
  165.4 52.7 %reduce-scatter.12.cloned.1.call-done = f32[512,1024]{1,0:T(8,128)} async-done(((f32[1024,1024]{1,0:T(8,128)}), f32[512,1024]{1,0:T(8,128)}) %reduce-scatter.12.cloned.1.call-update) | async-done | bytes 2097168 | tf_op jit(solution)/shard_map/reduce_scatter | solution.py:183
  225.5 48.4 %all-gather.20.cloned.1.call-done = bf16[1024,2304]{1,0:T(8,128)(2,1)} async-done(((bf16[64,2304]{1,0:T(8,128)(2,1)}), bf16[1024,2304]{1,0:T(8,128)(2,1)}) %all-gather.20.cloned.1.call-update) | async-done | bytes 4718608 | tf_op jit(solution)/shard_map/all_gather | solution.py:191
  274.0 33.7 %all-gather.16.cloned.1.call-done = bf16[1024,1024]{1,0:T(8,128)(2,1)} async-done(((bf16[512,1024]{1,0:T(8,128)(2,1)}), bf16[1024,1024]{1,0:T(8,128)(2,1)}) %all-gather.16.cloned.1.call-update) | async-done | bytes 2097168 | tf_op jit(solution)/shard_map/all_gather | solution.py:196
  307.7 10.4 fusion.132
  318.1 45.5 %all-gather.18.cloned.1.call-done = bf16[1024,2304]{1,0:T(8,128)(2,1)} async-done(((bf16[64,2304]{1,0:T(8,128)(2,1)}), bf16[1024,2304]{1,0:T(8,128)(2,1)}) %all-gather.18.cloned.1.call-update) | async-done | bytes 4718608 | tf_op jit(solution)/shard_map/all_gather | solution.py:190
  363.7 10.1 fusion.131
  373.7 23.8 %all-gather.24.cloned.1.call-done = bf16[1024,1024]{1,0:T(8,128)(2,1)} async-done(((bf16[512,1024]{1,0:T(8,128)(2,1)}), bf16[1024,1024]{1,0:T(8,128)(2,1)}) %all-gather.24.cloned.1.call-update) | async-done | bytes 2097168 | tf_op jit(solution)/shard_map/all_gather | solution.py:219
  397.6 56.0 %all-gather.22.cloned.1.call-done = bf16[2304,1024]{0,1:T(8,128)(2,1)} async-done(((bf16[2304,64]{0,1:T(8,128)(2,1)}), bf16[2304,1024]{0,1:T(8,128)(2,1)}) %all-gather.22.cloned.1.call-update) | async-done | bytes 4718608 | tf_op jit(solution)/shard_map/all_gather | solution.py:192
  453.5 18.0 %multiply_convert_fusion = (bf16[1024,2304]{1,0:T(8,128)(2,1)}, bf16[1024,2304]{1,0:T(8,128)(2,1)}, bf16[1024,2304]{1,0:T(8,128)(2,1)}) fusion(f32[1024,2304]{1,0:T(8,128)} %fusion.131, f32[1024,2304]{1,0:T(8,128)} %fusion.132, bf16[1024,1024]{1,0:T(8,128)(2,1)} %all-gather.24.cloned.1.call-done, bf16[2304,1024]{0,1:T(8,128)(2,1)} %all-gather.22.cloned.1.call-done), kind=kOutput, calls=%fused_computation.10 | convolution fusion | flops 4869586944 | bytes 39845888 | tf_op jit(solution)/shard_map/dot_general | solution.py:88
  487.5 30.3 %reduce-scatter.16.cloned.1.call-done = bf16[512,1024]{1,0:T(8,128)(2,1)} async-done(((bf16[1024,1024]{1,0:T(8,128)(2,1)}), bf16[512,1024]{1,0:T(8,128)(2,1)}) %reduce-scatter.16.cloned.1.call-update) | async-done | bytes 1048592 | tf_op jit(solution)/shard_map/reduce_scatter | solution.py:230
  545.1 12.1 %all-gather.26.cloned.1.call-done = bf16[1024,1024]{1,0:T(8,128)(2,1)} async-done(((bf16[512,1024]{1,0:T(8,128)(2,1)}), bf16[1024,1024]{1,0:T(8,128)(2,1)}) %all-gather.26.cloned.1.call-update) | async-done | bytes 2097168 | tf_op jit(solution)/shard_map/all_gather | solution.py:251
  646.0 9.8 convolution_convert_fusion.3
  658.2 57.3 %reduce-scatter.28.cloned.1.call-done = bf16[64,2304]{1,0:T(8,128)(2,1)} async-done(((bf16[1024,2304]{1,0:T(8,128)(2,1)}), bf16[64,2304]{1,0:T(8,128)(2,1)}) %reduce-scatter.28.cloned.1.call-update) | async-done | bytes 294928 | tf_op jit(solution)/shard_map/reduce_scatter | solution.py:241
  717.3 56.4 %reduce-scatter.24.cloned.1.call-done = bf16[64,256]{1,0:T(8,128)(2,1)} async-done(((bf16[1024,256]{1,0:T(8,128)(2,1)}), bf16[64,256]{1,0:T(8,128)(2,1)}) %reduce-scatter.24.cloned.1.call-update) | async-done | bytes 32784 | tf_op jit(solution)/shard_map/reduce_scatter | solution.py:347
  775.1 77.4 %reduce-scatter.32.cloned.1.call-done = bf16[2304,64]{0,1:T(8,128)(2,1)} async-done(((bf16[2304,1024]{0,1:T(8,128)(2,1)}), bf16[2304,64]{0,1:T(8,128)(2,1)}) %reduce-scatter.32.cloned.1.call-update) | async-done | bytes 294928 | tf_op jit(solution)/shard_map/reduce_scatter | solution.py:247
  854.4 56.5 %reduce-scatter.22.cloned.1.call-done = bf16[64,256]{1,0:T(8,128)(2,1)} async-done(((bf16[1024,256]{1,0:T(8,128)(2,1)}), bf16[64,256]{1,0:T(8,128)(2,1)}) %reduce-scatter.22.cloned.1.call-update) | async-done | bytes 32784 | tf_op jit(solution)/shard_map/reduce_scatter | solution.py:344
  912.2 59.0 %reduce-scatter.26.cloned.1.call-done = bf16[512,64]{0,1:T(8,128)(2,1)} async-done(((bf16[512,1024]{0,1:T(8,128)(2,1)}), bf16[512,64]{0,1:T(8,128)(2,1)}) %reduce-scatter.26.cloned.1.call-update) | async-done | bytes 65552 | tf_op jit(solution)/shard_map/reduce_scatter | solution.py:350
  972.7 59.0 %reduce-scatter.20.cloned.1.call-done = bf16[64,512]{1,0:T(8,128)(2,1)} async-done(((bf16[1024,512]{1,0:T(8,128)(2,1)}), bf16[64,512]{1,0:T(8,128)(2,1)}) %reduce-scatter.20.cloned.1.call-update) | async-done | bytes 65552 | tf_op jit(solution)/shard_map/reduce_scatter | solution.py:341
  1033.3 32.2 %reduce-scatter.18.cloned.1.call-done = bf16[512,1024]{1,0:T(8,128)(2,1)} async-done(((bf16[1024,1024]{1,0:T(8,128)(2,1)}), bf16[512,1024]{1,0:T(8,128)(2,1)}) %reduce-scatter.18.cloned.1.call-update) | async-done | bytes 1048592 | tf_op jit(solution)/shard_map/reduce_scatter | solution.py:330
  1067.6 39.8 %all-reduce.4 = (f32[1024]{0:T(1024)S(1)}, f32[64]{0:T(128)}, f32[64]{0:T(128)}, f32[1024]{0:T(1024)S(1)}) all-reduce(f32[1024]{0:T(1024)S(1)} %get-tuple-element.79, f32[64]{0:T(128)S(1)} %reduce_sum.193, f32[64]{0:T(128)S(1)} %reduce_sum.196, f32[1024]{0:T(1024)S(1)} %copy-done.59), channel_id=1, replica_groups=mesh['dp'=16,'tensor'=2] {'dp','tensor'}, use_global_device_ids=true, to_apply=%region_22.23 | all-reduce | flops 2176 | bytes 17408 | tf_op jit(solution)/shard_map/psum | solution.py:354
  (313 shorter events, 216.5 us)
Async XLA Ops:
  7.2 86.7 %all-gather.10.cloned.1.call-start = ((), (), s32[]{:S(2)}) async-start(), calls=%async_computation.11 | async-start | bytes 3145728 | tf_op jit(solution)/shard_map/all_gather | solution.py:132
  50.5 70.7 %all-gather.12.cloned.1.call-start = ((), (), s32[]{:S(2)}) async-start(), calls=%async_computation.12 | async-start | bytes 1114112 | tf_op jit(solution)/shard_map/all_gather | solution.py:124
  51.2 109.0 %all-gather.14.cloned.1.call-start = ((), (), s32[]{:S(2)}) async-start(), calls=%async_computation.13 | async-start | bytes 1114112 | tf_op jit(solution)/shard_map/all_gather | solution.py:127
  52.0 166.2 %reduce-scatter.12.cloned.1.call-start = ((), (), s32[]{:S(2)}) async-start(), calls=%async_computation.14 | async-start | bytes 6291456 | tf_op jit(solution)/shard_map/reduce_scatter | solution.py:183
  164.8 109.2 %all-gather.20.cloned.1.call-start = ((), (), s32[]{:S(2)}) async-start(), calls=%async_computation.17 | async-start | bytes 5013504 | tf_op jit(solution)/shard_map/all_gather | solution.py:191
  165.4 142.4 %all-gather.16.cloned.1.call-start = ((), (), s32[]{:S(2)}) async-start(), calls=%async_computation.15 | async-start | bytes 3145728 | tf_op jit(solution)/shard_map/all_gather | solution.py:196
  221.6 142.1 %all-gather.18.cloned.1.call-start = ((), (), s32[]{:S(2)}) async-start(), calls=%async_computation.16 | async-start | bytes 5013504 | tf_op jit(solution)/shard_map/all_gather | solution.py:190
  222.3 175.2 %all-gather.24.cloned.1.call-start = ((), (), s32[]{:S(2)}) async-start(), calls=%async_computation.20 | async-start | bytes 3145728 | tf_op jit(solution)/shard_map/all_gather | solution.py:219
  224.7 228.8 %all-gather.22.cloned.1.call-start = ((), (), s32[]{:S(2)}) async-start(), calls=%async_computation.18 | async-start | bytes 5013504 | tf_op jit(solution)/shard_map/all_gather | solution.py:192
  225.5 292.3 %reduce-scatter.16.cloned.1.call-start = ((), (), s32[]{:S(2)}) async-start(), calls=%async_computation.21 | async-start | bytes 3145728 | tf_op jit(solution)/shard_map/reduce_scatter | solution.py:230
  487.3 69.9 %all-gather.26.cloned.1.call-start = ((), (), s32[]{:S(2)}) async-start(), calls=%async_computation.22 | async-start | bytes 3145728 | tf_op jit(solution)/shard_map/all_gather | solution.py:251
  523.9 132.2 %reduce-scatter.30.cloned.1.call-start = ((), (), s32[]{:S(2)}) async-start(), calls=%async_computation.29 | async-start | bytes 5013504 | tf_op jit(solution)/shard_map/reduce_scatter | solution.py:244
  533.5 182.0 %reduce-scatter.28.cloned.1.call-start = ((), (), s32[]{:S(2)}) async-start(), calls=%async_computation.28 | async-start | bytes 5013504 | tf_op jit(solution)/shard_map/reduce_scatter | solution.py:241
  544.3 229.4 %reduce-scatter.24.cloned.1.call-start = ((), (), s32[]{:S(2)}) async-start(), calls=%async_computation.26 | async-start | bytes 557056 | tf_op jit(solution)/shard_map/reduce_scatter | solution.py:347
  574.7 277.8 %reduce-scatter.32.cloned.1.call-start = ((), (), s32[]{:S(2)}) async-start(), calls=%async_computation.30 | async-start | bytes 5013504 | tf_op jit(solution)/shard_map/reduce_scatter | solution.py:247
  584.7 326.1 %reduce-scatter.22.cloned.1.call-start = ((), (), s32[]{:S(2)}) async-start(), calls=%async_computation.25 | async-start | bytes 557056 | tf_op jit(solution)/shard_map/reduce_scatter | solution.py:344
  622.9 348.4 %reduce-scatter.26.cloned.1.call-start = ((), (), s32[]{:S(2)}) async-start(), calls=%async_computation.27 | async-start | bytes 1114112 | tf_op jit(solution)/shard_map/reduce_scatter | solution.py:350
  632.1 399.7 %reduce-scatter.20.cloned.1.call-start = ((), (), s32[]{:S(2)}) async-start(), calls=%async_computation.24 | async-start | bytes 1114112 | tf_op jit(solution)/shard_map/reduce_scatter | solution.py:341
  641.4 424.1 %reduce-scatter.18.cloned.1.call-start = ((), (), s32[]{:S(2)}) async-start(), calls=%async_computation.23 | async-start | bytes 3145728 | tf_op jit(solution)/shard_map/reduce_scatter | solution.py:330
  645.9 462.6 %reduce-scatter.14.cloned.1.call-start = ((), (), s32[]{:S(2)}) async-start(), calls=%async_computation.19 | async-start | bytes 3145728 | tf_op jit(solution)/shard_map/reduce_scatter | solution.py:200
  655.8 452.8 %copy-start.2 = (f32[512,1024]{1,0:T(8,128)S(1)}, f32[512,1024]{1,0:T(8,128)}, u32[]{:S(2)}) copy-start(f32[512,1024]{1,0:T(8,128)} %copy-done.1) | copy-start | bytes 6291460
  655.8 452.8 %copy-start.46 = (f32[1024]{0:T(1024)S(1)}, f32[1024]{0:T(1024)}, u32[]{:S(2)}) copy-start(f32[1024]{0:T(1024)} %copy-done.45) | copy-start | bytes 12292
  655.8 452.8 %copy-start.50 = (f32[512]{0:T(512)S(1)}, f32[512]{0:T(512)}, u32[]{:S(2)}) copy-start(f32[512]{0:T(512)} %copy-done.49) | copy-start | bytes 6148
  655.8 452.8 %copy-start.56 = (f32[512]{0:T(512)S(1)}, f32[512]{0:T(512)}, u32[]{:S(2)}) copy-start(f32[512]{0:T(512)} %copy-done.55) | copy-start | bytes 6148
  (79 other events, 4918.2 us)
Sparse Core Ops, SparseCore 0:
  50.6 30.3 all-gather.9
  83.2 37.9 all-gather.11
  123.3 36.8 all-gather.13
  164.9 53.2 reduce-scatter.11
  220.5 53.3 all-gather.19
  276.0 31.6 all-gather.15
  310.2 53.3 all-gather.17
  365.9 31.6 all-gather.23
  400.1 53.3 all-gather.21
  487.4 30.3 reduce-scatter.15
  524.0 33.1 all-gather.25
  560.9 75.5 reduce-scatter.29
  640.8 74.5 reduce-scatter.27
  718.9 54.8 reduce-scatter.23
  777.9 74.5 reduce-scatter.31
  856.0 54.8 reduce-scatter.21
  914.7 56.4 reduce-scatter.25
  975.3 56.4 reduce-scatter.19
  1034.7 30.7 reduce-scatter.17
  1067.6 32.4 reduce-scatter.13
where the time goes:
time: 1130 us; the launch traced here: 1120 us
  waiting for transfers between devices  737 us (65%)
  matrix products  176 us (16%)
  blocking collectives  114 us (10%)
  other arithmetic  53.2 us (5%)
  local copies, waits for them, and re-layouts  21.2 us (2%)
  between operations  16.6 us (1%)
    reduce_scatter x1, waiting for transfers between devices, per_device(): lax.psum_scatter(grad_down.astype(jnp.bfloat16), 'dp', scatter_dimension=...  77.4 us
    reduce_scatter x1, waiting for transfers between devices, per_device(): lax.psum_scatter(grad_wq.astype(jnp.bfloat16), 'dp', scatter_dimension=0,...  59 us
    reduce_scatter x1, waiting for transfers between devices, per_device(): lax.psum_scatter(grad_wo.astype(jnp.bfloat16), 'dp', scatter_dimension=1,...  59 us
    reduce_scatter x1, waiting for transfers between devices, per_device(): lax.psum_scatter(grad_gate_w.astype(jnp.bfloat16), 'dp', scatter_dimensio...  57.3 us
    reduce_scatter x1, waiting for transfers between devices, per_device(): lax.psum_scatter(grad_wk.astype(jnp.bfloat16), 'dp', scatter_dimension=0,...  56.5 us
    reduce_scatter x1, waiting for transfers between devices, per_device(): lax.psum_scatter(grad_wv.astype(jnp.bfloat16), 'dp', scatter_dimension=0,...  56.4 us
    all_gather x1, waiting for transfers between devices, per_device(): lax.all_gather(w_down, 'dp', axis=1, tiled=True)  56 us
    reduce_scatter x1, waiting for transfers between devices, per_device(): lax.psum_scatter(jnp.dot(heads_low, wo_all, preferred_element_type=jnp.fl...  52.7 us
  transfers between devices with their start and end apart: 20, of which 17 were waited for; matrix products, arithmetic and copies ran while one was open for 16% of the time, Pallas kernels for 0%

commit v1 on v0

--- a/solution.py
+++ b/solution.py
@@ -88,6 +88,130 @@
     return lax.dot_general(
         left, right, (((1,), (1,)), ((), ())), preferred_element_type=jnp.float32
     )
+
+
+def ring_pos(chip, chips):
+    return jnp.where(chip % 2 == 0, chip // 2, chips - 1 - chip // 2)
+
+
+def ring_chip(pos, chips):
+    pos = pos % chips
+    return jnp.where(pos < chips // 2, 2 * pos, 2 * (chips - 1 - pos) + 1)
+
+
+def ring_perms(chips):
+    order = list(range(0, chips, 2)) + list(range(1, chips, 2))[::-1]
+    right = []
+    for place in range(chips):
+        for core in range(2):
+            right.append((order[place] * 2 + core, order[(place + 1) % chips] * 2 + core))
+    return right, [(b, a) for a, b in right], [(i, i ^ 1) for i in range(2 * chips)]
+
+
+def hops(chips, flip):
+    longer = chips // 2
+    return (chips - 1 - longer, longer) if flip else (longer, chips - 1 - longer)
+
+
+def ring_gather(block, flip):
+    chips = lax.axis_size("dp") // 2
+    right, left, sibling = ring_perms(chips)
+    index = lax.axis_index("dp")
+    core = index % 2
+    place = ring_pos(index // 2, chips)
+    count_right, count_left = hops(chips, flip)
+    lane = jnp.zeros((chips,) + block.shape, block.dtype)
+    lane = lax.dynamic_update_index_in_dim(lane, block, index // 2, 0)
+    from_left, from_right = block, block
+    for step in range(1, max(count_right, count_left) + 1):
+        if step <= count_right:
+            from_left = lax.ppermute(from_left, "dp", right)
+            lane = lax.dynamic_update_index_in_dim(
+                lane, from_left, ring_chip(place - step, chips), 0
+            )
+        if step <= count_left:
+            from_right = lax.ppermute(from_right, "dp", left)
+            lane = lax.dynamic_update_index_in_dim(
+                lane, from_right, ring_chip(place + step, chips), 0
+            )
+    other = lax.ppermute(lane, "dp", sibling)
+    first = jnp.where(core == 0, lane, other)
+    second = jnp.where(core == 0, other, lane)
+    return jnp.stack([first, second], axis=1).reshape(2 * chips * block.shape[0], -1)
+
+
+def ring_scatter(full, flip):
+    chips = lax.axis_size("dp") // 2
+    right, left, sibling = ring_perms(chips)
+    index = lax.axis_index("dp")
+    core = index % 2
+    place = ring_pos(index // 2, chips)
+    count_right, count_left = hops(chips, flip)
+    pairs = full.reshape(chips, 2, full.shape[0] // (2 * chips), full.shape[1])
+    mine = jnp.where(core == 0, pairs[:, 0], pairs[:, 1])
+    theirs = jnp.where(core == 0, pairs[:, 1], pairs[:, 0])
+    got = lax.ppermute(theirs, "dp", sibling)
+
+    def chunk(pos):
+        chip = ring_chip(pos, chips)
+        return lax.dynamic_index_in_dim(mine, chip, 0, keepdims=False).astype(
+            jnp.float32
+        ) + lax.dynamic_index_in_dim(got, chip, 0, keepdims=False).astype(jnp.float32)
+
+    total = chunk(place)
+    for count, perm, sign in ((count_right, right, 1), (count_left, left, -1)):
+        received = None
+        for step in range(count, 0, -1):
+            partial = chunk(place + sign * step)
+            if received is not None:
+                partial = partial + received.astype(jnp.float32)
+            received = lax.ppermute(partial.astype(jnp.bfloat16), "dp", perm)
+        if received is not None:
+            total = total + received.astype(jnp.float32)
+    return total
+
+
+def shifted(values, shift):
+    size = lax.axis_size("tensor")
+    return lax.ppermute(values, "tensor", [((i + shift) % size, i) for i in range(size)])
+
+
+def gather_parts(own):
+    return [own] + [shifted(own, k) for k in range(1, lax.axis_size("tensor"))]
+
+
+def scatter_parts(make_part):
+    size = lax.axis_size("tensor")
+    arrived = [shifted(make_part(k).astype(jnp.bfloat16), -k) for k in range(1, size)]
+    total = make_part(0)
+    for part in arrived:
+        total = total + part.astype(jnp.float32)
+    return total
+
+
+def to_slots(parts):
+    size = len(parts)
+    rows = parts[0].shape[0]
+    start = ((size - lax.axis_index("tensor")) % size) * rows
+    return lax.dynamic_slice_in_dim(jnp.concatenate(parts + parts[:-1], axis=0), start, size * rows, 0)
+
+
+def part_of(values, k):
+    size = lax.axis_size("tensor")
+    rows = values.shape[0] // size
+    return lax.dynamic_slice_in_dim(
+        values, ((lax.axis_index("tensor") + k) % size) * rows, rows, 0
+    )
+
+
+def sum_everywhere(values):
+    for name in ("tensor", "dp"):
+        size = lax.axis_size(name)
+        bit = 1
+        while bit < size:
+            values = values + lax.ppermute(values, name, [(i, i ^ bit) for i in range(size)])
+            bit *= 2
+    return values
 
 
 def per_device(
@@ -120,16 +244,36 @@
     cosine_table, sine_table = rope_tables(position, head_dim)
     qgain_wide = query_gain.astype(jnp.float32)
     kgain_wide = key_gain.astype(jnp.float32)
-    wq_all, wk_all, wv_all, wo_all, attn_gain_all = (
-        lax.all_gather(w_query, "dp", axis=0, tiled=True),
-        lax.all_gather(key_weight, "dp", axis=0, tiled=True),
-        lax.all_gather(value_weight, "dp", axis=0, tiled=True),
-        lax.all_gather(w_out, "dp", axis=1, tiled=True),
-        lax.all_gather(attn_gain, "dp", axis=0, tiled=True),
-    )
+    shard_rows = w_query.shape[0]
+    qw, kw = w_query.shape[1], key_weight.shape[1]
+    token_parts = gather_parts(tokens)
+    grad_out = jnp.where(valid_local[:, None], out_grad, jnp.zeros_like(out_grad))
+    gain_columns = jnp.concatenate(
+        [
+            attn_gain[:, None],
+            ffn_gain[:, None],
+            jnp.zeros((shard_rows, 126), jnp.bfloat16),
+        ],
+        axis=1,
+    )
+    attn_pack = ring_gather(
+        jnp.concatenate([w_query, key_weight, value_weight, w_out.T, gain_columns], axis=1), False
+    )
+    wg_all = ring_gather(w_gate, True)
+    wu_all = ring_gather(w_up, False)
+    wdt_all = ring_gather(w_down.T, True)
+    wq_all = attn_pack[:, :qw]
+    wk_all = attn_pack[:, qw : qw + kw]
+    wv_all = attn_pack[:, qw + kw : qw + 2 * kw]
+    wot_all = attn_pack[:, qw + 2 * kw : 2 * qw + 2 * kw]
+    attn_gain_all = attn_pack[:, 2 * qw + 2 * kw]
+    ffn_gain_all = attn_pack[:, 2 * qw + 2 * kw + 1]
+    grad_parts = gather_parts(grad_out)
     tokens_wide = tokens.astype(jnp.float32)
-    attn_in, attn_inv = rows_normalize(tokens_wide, attn_gain_all.astype(jnp.float32))
-    attn_rows = lax.all_gather(attn_in.astype(jnp.bfloat16), "tensor", axis=0, tiled=True)
+    attn_inv = lax.rsqrt(jnp.mean(tokens_wide * tokens_wide, axis=-1, keepdims=True) + EPSILON)
+    attn_rows = rows_normalize(
+        to_slots(token_parts).astype(jnp.float32), attn_gain_all.astype(jnp.float32)
+    )[0].astype(jnp.bfloat16)
     query_raw = jnp.dot(attn_rows, wq_all, preferred_element_type=jnp.float32).reshape(
         group_rows, query_heads, head_dim
     )
@@ -180,81 +324,52 @@
         .reshape(group_rows, query_heads * head_dim)
         .astype(jnp.bfloat16)
     )
-    mixed = tokens_wide + lax.psum_scatter(
-        jnp.dot(heads_low, wo_all, preferred_element_type=jnp.float32),
-        "tensor",
-        scatter_dimension=0,
-        tiled=True,
-    )
-    wg_all, wu_all, wd_all, ffn_gain_all = (
-        lax.all_gather(w_gate, "dp", axis=0, tiled=True),
-        lax.all_gather(w_up, "dp", axis=0, tiled=True),
-        lax.all_gather(w_down, "dp", axis=1, tiled=True),
-        lax.all_gather(ffn_gain, "dp", axis=0, tiled=True),
-    )
+    mixed = tokens_wide + scatter_parts(lambda k: contract_cols(part_of(heads_low, k), wot_all))
     ffn_in, ffn_inv = rows_normalize(mixed, ffn_gain_all.astype(jnp.float32))
-    ffn_rows = lax.all_gather(ffn_in.astype(jnp.bfloat16), "tensor", axis=0, tiled=True)
-    gate = jnp.dot(ffn_rows, wg_all, preferred_element_type=jnp.float32)
-    up_proj = jnp.dot(ffn_rows, wu_all, preferred_element_type=jnp.float32)
-    hidden = (jax.nn.silu(gate) * up_proj).astype(jnp.bfloat16)
-    result = mixed + lax.psum_scatter(
-        jnp.dot(hidden, wd_all, preferred_element_type=jnp.float32).astype(jnp.bfloat16),
-        "tensor",
-        scatter_dimension=0,
-        tiled=True,
-    ).astype(jnp.float32)
-    output = result.astype(jnp.bfloat16)
-    wq_all, wk_all, wv_all, wo_all, attn_gain_all, wg_all, wu_all, wd_all, ffn_gain_all = (
-        lax.all_gather(w_query, "dp", axis=0, tiled=True),
-        lax.all_gather(key_weight, "dp", axis=0, tiled=True),
-        lax.all_gather(value_weight, "dp", axis=0, tiled=True),
-        lax.all_gather(w_out, "dp", axis=1, tiled=True),
-        lax.all_gather(attn_gain, "dp", axis=0, tiled=True),
-        lax.all_gather(w_gate, "dp", axis=0, tiled=True),
-        lax.all_gather(w_up, "dp", axis=0, tiled=True),
-        lax.all_gather(w_down, "dp", axis=1, tiled=True),
-        lax.all_gather(ffn_gain, "dp", axis=0, tiled=True),
-    )
-    grad_out = jnp.where(valid_local[:, None], out_grad, jnp.zeros_like(out_grad))
-    grad_rows = lax.all_gather(grad_out, "tensor", axis=0, tiled=True)
-    grad_hidden = contract_cols(grad_rows, wd_all)
-    grad_down = contract_rows(hidden, grad_rows)
-    sigmoid_gate = jax.nn.sigmoid(gate)
-    grad_up_low = (grad_hidden * gate * sigmoid_gate).astype(jnp.bfloat16)
-    grad_gate_low = (
-        grad_hidden * up_proj * sigmoid_gate * (1.0 + gate * (1.0 - sigmoid_gate))
-    ).astype(jnp.bfloat16)
-    grad_gate_w = contract_rows(ffn_rows, grad_gate_low)
-    grad_up_w = contract_rows(ffn_rows, grad_up_low)
-    gate_part = contract_cols(grad_gate_low, wg_all)
-    grad_ffn_in = lax.psum_scatter(
-        (gate_part + contract_cols(grad_up_low, wu_all)).astype(jnp.bfloat16),
-        "tensor",
-        scatter_dimension=0,
-        tiled=True,
-    ).astype(jnp.float32)
+    ffn_parts = gather_parts(ffn_in.astype(jnp.bfloat16))
+    gates, ups, hiddens, grad_gates, grad_ups = [], [], [], [], []
+    for ffn_rows, grad_rows in zip(ffn_parts, grad_parts):
+        gate = jnp.dot(ffn_rows, wg_all, preferred_element_type=jnp.float32)
+        up_proj = jnp.dot(ffn_rows, wu_all, preferred_element_type=jnp.float32)
+        grad_hidden = jnp.dot(grad_rows, wdt_all, preferred_element_type=jnp.float32)
+        sigmoid_gate = jax.nn.sigmoid(gate)
+        hiddens.append((gate * sigmoid_gate * up_proj).astype(jnp.bfloat16))
+        grad_ups.append((grad_hidden * gate * sigmoid_gate).astype(jnp.bfloat16))
+        grad_gates.append(
+            (
+                grad_hidden * up_proj * sigmoid_gate * (1.0 + gate * (1.0 - sigmoid_gate))
+            ).astype(jnp.bfloat16)
+        )
+    grad_ffn_in = scatter_parts(
+        lambda k: contract_cols(grad_gates[k], wg_all) + contract_cols(grad_ups[k], wu_all)
+    )
     back_mixed, ffn_gain_part = norm_back(
         mixed, ffn_inv, ffn_gain_all.astype(jnp.float32), grad_ffn_in
     )
     grad_mixed = grad_out.astype(jnp.float32) + back_mixed
+    mixed_parts = gather_parts(grad_mixed.astype(jnp.bfloat16))
+    result = mixed + scatter_parts(lambda k: contract_cols(hiddens[k], wdt_all))
+    output = result.astype(jnp.bfloat16)
+    ffn_cat = jnp.concatenate(ffn_parts, axis=0)
+    grad_cat = jnp.concatenate(grad_parts, axis=0)
     ffn_sums = (
-        lax.psum_scatter(
-            grad_gate_w.astype(jnp.bfloat16), "dp", scatter_dimension=0, tiled=True
-        ).astype(jnp.float32),
-        lax.psum_scatter(
-            grad_up_w.astype(jnp.bfloat16), "dp", scatter_dimension=0, tiled=True
-        ).astype(jnp.float32),
-        lax.psum_scatter(
-            grad_down.astype(jnp.bfloat16), "dp", scatter_dimension=1, tiled=True
-        ).astype(jnp.float32),
-    )
-    grad_mixed_rows = lax.all_gather(grad_mixed.astype(jnp.bfloat16), "tensor", axis=0, tiled=True)
-    grad_heads = (
-        contract_cols(grad_mixed_rows, wo_all)
-        .astype(jnp.bfloat16)
-        .reshape(group_rows, kv_heads, repeat, head_dim)
-    )
-    grad_wo = contract_rows(heads_low, grad_mixed_rows)
+        ring_scatter(
+            contract_rows(ffn_cat, jnp.concatenate(grad_gates, axis=0)).astype(jnp.bfloat16), False
+        ),
+        ring_scatter(
+            contract_rows(ffn_cat, jnp.concatenate(grad_ups, axis=0)).astype(jnp.bfloat16), True
+        ),
+        ring_scatter(
+            contract_rows(grad_cat, jnp.concatenate(hiddens, axis=0)).astype(jnp.bfloat16), False
+        ).T,
+    )
+    grad_heads = to_slots(
+        [
+            jnp.dot(rows, wot_all, preferred_element_type=jnp.float32).astype(jnp.bfloat16)
+            for rows in mixed_parts
+        ]
+    ).reshape(group_rows, kv_heads, repeat, head_dim)
+    grad_wot = contract_rows(to_slots(mixed_parts), heads_low)
     grad_query_parts = []
     grad_key = jnp.zeros((group_rows, kv_heads, head_dim), jnp.float32)
     grad_value = jnp.zeros((group_rows, kv_heads, head_dim), jnp.float32)
@@ -324,41 +439,39 @@
     grad_wq = contract_rows(attn_rows, grad_query_low)
     grad_wk = contract_rows(attn_rows, grad_key_low)
     grad_wv = contract_rows(attn_rows, grad_value_low)
-    query_part = contract_cols(grad_query_low, wq_all)
-    key_part = contract_cols(grad_key_low, wk_all)
-    value_part = contract_cols(grad_value_low, wv_all)
-    grad_attn_in = lax.psum_scatter(
-        (query_part + key_part + value_part).astype(jnp.bfloat16),
-        "tensor",
-        scatter_dimension=0,
-        tiled=True,
-    ).astype(jnp.float32)
+    grad_attn_in = scatter_parts(
+        lambda k: contract_cols(part_of(grad_query_low, k), wq_all)
+        + contract_cols(part_of(grad_key_low, k), wk_all)
+        + contract_cols(part_of(grad_value_low, k), wv_all)
+    )
     back_tokens, attn_gain_part = norm_back(
         tokens_wide, attn_inv, attn_gain_all.astype(jnp.float32), grad_attn_in
     )
     input_grad = grad_mixed + back_tokens
+    attn_pack_sum = ring_scatter(
+        jnp.concatenate([grad_wq, grad_wk, grad_wv, grad_wot], axis=1).astype(jnp.bfloat16), True
+    )
     attn_sums = (
-        lax.psum_scatter(
-            grad_wq.astype(jnp.bfloat16), "dp", scatter_dimension=0, tiled=True
-        ).astype(jnp.float32),
-        lax.psum_scatter(
-            grad_wk.astype(jnp.bfloat16), "dp", scatter_dimension=0, tiled=True
-        ).astype(jnp.float32),
-        lax.psum_scatter(
-            grad_wv.astype(jnp.bfloat16), "dp", scatter_dimension=0, tiled=True
-        ).astype(jnp.float32),
-        lax.psum_scatter(
-            grad_wo.astype(jnp.bfloat16), "dp", scatter_dimension=1, tiled=True
-        ).astype(jnp.float32),
-    )
-    gain_sums = lax.psum(
-        (
-            jnp.sum(attn_gain_part, axis=0),
-            jnp.sum(ffn_gain_part, axis=0),
-            jnp.sum(qgain_terms, axis=(0, 1)),
-            jnp.sum(kgain_terms, axis=(0, 1)),
-        ),
-        ("dp", "tensor"),
+        attn_pack_sum[:, :qw],
+        attn_pack_sum[:, qw : qw + kw],
+        attn_pack_sum[:, qw + kw : qw + 2 * kw],
+        attn_pack_sum[:, qw + 2 * kw :].T,
+    )
+    width = tokens.shape[1]
+    early = sum_everywhere(
+        jnp.concatenate(
+            [
+                jnp.sum(ffn_gain_part, axis=0),
+                jnp.sum(qgain_terms, axis=(0, 1)),
+                jnp.sum(kgain_terms, axis=(0, 1)),
+            ]
+        )
+    )
+    gain_sums = (
+        sum_everywhere(jnp.sum(attn_gain_part, axis=0)),
+        early[:width],
+        early[width : width + head_dim],
+        early[width + head_dim :],
     )
     gain_shard = attn_gain.shape[0]
     gain_start = lax.axis_index("dp") * gain_shard

time: 1130 us -> 608 us (0.54)
  waiting for transfers between devices: 737 us -> 186 us
  blocking collectives: 114 us -> 0 us
  starting transfers between devices: 1.45 us -> 80.4 us
  other arithmetic: 53.2 us -> 101 us
  local copies, waits for them, and re-layouts: 21.2 us -> 56.1 us
  between operations: 16.6 us -> 2.48 us
    reduce_scatter x11 -> x0, waiting for transfers between devices: 481 us -> none  [the longest x1 77.4 us: per_device(): lax.psum_scatter(grad_down.astype(jnp.bfloat16), 'dp', scatter_dimension=...]
    all_gather x9 -> x0, waiting for transfers between devices: 252 us -> none  [the longest x1 56 us: per_device(): lax.all_gather(w_down, 'dp', axis=1, tiled=True)]
    ppermute x0 -> x82, waiting for transfers between devices: none -> 186 us  [the longest x28 67.6 us: ring_scatter(): received = lax.ppermute(partial.astype(jnp.bfloat16), 'dp', perm)]
    ppermute x0 -> x82, starting transfers between devices: none -> 80.4 us  [the longest x28 26.2 us: ring_scatter(): received = lax.ppermute(partial.astype(jnp.bfloat16), 'dp', perm)]
    psum x1 -> x0, blocking collectives: 39.8 us -> none  [per_device(): lax.psum((jnp.sum(attn_gain_part, axis=0), jnp.sum(ffn_gain_part, axis=0)...]
    all_gather x2 -> x0, blocking collectives: 39.7 us -> none  [the longest x1 21 us: per_device(): lax.all_gather(value_weight, 'dp', axis=0, tiled=True)]
    unnamed x1 -> x0, blocking collectives: 34.9 us -> none
    dynamic_update_slice x0 -> x32, local copies, waits for them, and re-layouts: none -> 22.7 us  [the longest x14 11.1 us: ring_gather(): lax.dynamic_update_index_in_dim(lane, from_right, ring_chip(place + step,...]
  transfers between devices with their start and end apart: 20 -> 82, of which waited for: 17 -> 39; matrix products, arithmetic and copies ran while one was open for 16% -> 50% of each run, Pallas kernels for 0% -> 0%
where the time goes in v1:
time: 608 us; the launch traced here: 601 us
  waiting for transfers between devices  186 us (31%)
  matrix products  175 us (29%)
  other arithmetic  101 us (17%)
  starting transfers between devices  80.4 us (13%)
  local copies, waits for them, and re-layouts  56.1 us (9%)
    ppermute x28, waiting for transfers between devices, ring_scatter(): received = lax.ppermute(partial.astype(jnp.bfloat16), 'dp', perm)  67.6 us
    ppermute x14, waiting for transfers between devices, ring_gather(): from_left = lax.ppermute(from_left, 'dp', right)  45.7 us
    ppermute x8, waiting for transfers between devices, shifted(): lax.ppermute(values, 'tensor', [((i + shift) % size, i) for i in range(si...  39.5 us
    dot_general x14, matrix products, contract_cols(): lax.dot_general(left, right, (((1,), (1,)), ((), ())), preferred_element_...  32.9 us
    ppermute x28, starting transfers between devices, ring_scatter(): received = lax.ppermute(partial.astype(jnp.bfloat16), 'dp', perm)  26.2 us
    dot_general x7, matrix products, contract_rows(): lax.dot_general(left, right, (((0,), (0,)), ((), ())), preferred_element_...  24.7 us
    convert_element_type x20, other arithmetic, ring_scatter(): received = lax.ppermute(partial.astype(jnp.bfloat16), 'dp', perm)  23.4 us
    ppermute x14, waiting for transfers between devices, ring_gather(): from_right = lax.ppermute(from_right, 'dp', left)  20.2 us
  transfers between devices with their start and end apart: 82, of which 39 were waited for; matrix products, arithmetic and copies ran while one was open for 50% of the time, Pallas kernels for 0%

profile of v1, /device:TPU:0, one launch (start us, length us, event | category | flops | bytes accessed | tf_op | source)
XLA Modules:
  0.0 600.9 jit_solution(5676392202282599735)
XLA Ops:
  36.8 9.6 %collective-permute-done.18 = bf16[64,2304]{1,0:T(8,128)(2,1)S(1)} collective-permute-done((bf16[64,2304]{1,0:T(8,128)(2,1)S(1)}, bf16[64,2304]{1,0:T(8,128)(2,1)S(1)}, u32[]{:S(2)}, u32[]{:S(2)}) %collective-permute-start.18) | collective-permute-done | bytes 294944 | tf_op jit(solution)/shard_map/ppermute | solution.py:128
  70.4 6.8 %collective-permute-done.20 = bf16[64,2304]{1,0:T(8,128)(2,1)S(1)} collective-permute-done((bf16[64,2304]{1,0:T(8,128)(2,1)S(1)}, bf16[64,2304]{1,0:T(8,128)(2,1)S(1)}, u32[]{:S(2)}, u32[]{:S(2)}) %collective-permute-start.20) | collective-permute-done | bytes 294944 | tf_op jit(solution)/shard_map/ppermute | solution.py:128
  79.9 6.7 %collective-permute-done.21 = bf16[64,2304]{1,0:T(8,128)(2,1)S(1)} collective-permute-done((bf16[64,2304]{1,0:T(8,128)(2,1)S(1)}, bf16[64,2304]{1,0:T(8,128)(2,1)S(1)}, u32[]{:S(2)}, u32[]{:S(2)}) %collective-permute-start.21) | collective-permute-done | bytes 294944 | tf_op jit(solution)/shard_map/ppermute | solution.py:133
  93.2 6.4 %collective-permute-done.12 = bf16[64,2304]{1,0:T(8,128)(2,1)S(1)} collective-permute-done((bf16[64,2304]{1,0:T(8,128)(2,1)S(1)}, bf16[64,2304]{1,0:T(8,128)(2,1)S(1)}, u32[]{:S(2)}, u32[]{:S(2)}) %collective-permute-start.12) | collective-permute-done | bytes 294944 | tf_op jit(solution)/shard_map/ppermute | solution.py:128
  101.1 6.4 %collective-permute-done.5 = bf16[64,1664]{1,0:T(8,128)(2,1)S(1)} collective-permute-done((bf16[64,1664]{1,0:T(8,128)(2,1)S(1)}, bf16[64,1664]{1,0:T(8,128)(2,1)S(1)}, u32[]{:S(2)}, u32[]{:S(2)}) %collective-permute-start.5) | collective-permute-done | bytes 213024 | tf_op jit(solution)/shard_map/ppermute | solution.py:128
  136.1 9.2 %collective-permute-done.16 = bf16[64,2304]{1,0:T(8,128)(2,1)S(1)} collective-permute-done((bf16[64,2304]{1,0:T(8,128)(2,1)S(1)}, bf16[64,2304]{1,0:T(8,128)(2,1)S(1)}, u32[]{:S(2)}, u32[]{:S(2)}) %collective-permute-start.16) | collective-permute-done | bytes 294944 | tf_op jit(solution)/shard_map/ppermute | solution.py:133
  156.8 11.2 %fusion.263 = (f32[4,2,512]{2,1,0:T(2,128)S(1)}, f32[4,2,512,1024]{2,3,1,0:T(8,128)}) fusion(pred[512,1024]{0,1:T(8,128)(4,1)} %fusion.58, bf16[512,4,2,64]{0,3,2,1:T(8,128)(2,1)} %bitcast.672, bf16[1024,4,32]{0,2,1:T(8,128)(2,1)} %get-tuple-element.139, bf16[1024,4,32]{0,2,1:T(8,128)(2,1)} %get-tuple-element.138), kind=kOutput, calls=%fused_computation.443 | convolution fusion | flops 554697728 | bytes 18366464 | tf_op jit(solution)/shard_map/sub | solution.py:310
  168.0 8.4 %fusion.75 = bf16[4,64,2,512]{3,1,2,0:T(8,128)(2,1)} fusion(bf16[1024,4,64,1]{0,2,3,1:T(8,128)(2,1)} %bitcast.693, f32[4,2,512,1024]{2,3,1,0:T(8,128)} %get-tuple-element.164, f32[4,2,512]{2,1,0:T(2,128)S(1)} %get-tuple-element.163), kind=kOutput, calls=%fused_computation.161 | convolution fusion | flops 545521664 | bytes 17842176 | tf_op jit(solution)/shard_map/grqk,kgd->qgrd/dot_general | solution.py:314
  177.1 7.7 %fusion.268 = (f32[4,2,512]{2,1,0:T(2,128)S(1)}, f32[4,2,512,512]{2,3,1,0:T(8,128)}) fusion(pred[512,512]{0,1:T(8,128)(4,1)} %fusion.95, bf16[512,4,2,64]{0,3,2,1:T(8,128)(2,1)} %bitcast.668, bf16[1024,4,32]{0,2,1:T(8,128)(2,1)} %get-tuple-element.138, bf16[1024,4,32]{0,2,1:T(8,128)(2,1)} %get-tuple-element.139), kind=kOutput, calls=%fused_computation.444 | convolution fusion | flops 277348864 | bytes 9715712 | tf_op jit(solution)/shard_map/sub | solution.py:310
  209.4 6.0 fusion.275
  215.8 6.3 %fusion.277 = f32[512,2304]{1,0:T(8,128)} fusion(bf16[512,1024]{1,0:T(8,128)(2,1)} %collective-permute-done.36, bf16[1024,2304]{1,0:T(8,128)(2,1)S(1)} %bitcast.652), kind=kOutput, calls=%fused_computation.449 | convolution fusion | flops 2415919104 | bytes 10485760 | tf_op jit(solution)/shard_map/dot_general | solution.py:334
  228.9 8.3 %multiply_convert_fusion.2 = (bf16[512,2304]{1,0:T(8,128)(2,1)}, bf16[512,2304]{1,0:T(8,128)(2,1)}, bf16[512,2304]{1,0:T(8,128)(2,1)}) fusion(f32[512,2304]{1,0:T(8,128)S(1)} %bitcast.703, f32[512,2304]{1,0:T(8,128)} %fusion.273, bf16[512,1024]{1,0:T(8,128)(2,1)S(1)} %multiply_convert_fusion.6, bf16[1024,2304]{1,0:T(8,128)(2,1)S(1)} %bitcast.657), kind=kOutput, calls=%fused_computation.45 | convolution fusion | flops 2434793472 | bytes 22282240 | tf_op jit(solution)/shard_map/dot_general | solution.py:332
  237.2 5.8 fusion.276
  253.0 8.6 %multiply_convert_fusion.1 = (bf16[512,2304]{1,0:T(8,128)(2,1)}, bf16[512,2304]{1,0:T(8,128)(2,1)}, bf16[512,2304]{1,0:T(8,128)(2,1)}) fusion(f32[512,2304]{1,0:T(8,128)S(1)} %bitcast.701, f32[512,2304]{1,0:T(8,128)} %fusion.274, bf16[512,1024]{1,0:T(8,128)(2,1)S(1)} %collective-permute-done.34, bf16[1024,2304]{1,0:T(8,128)(2,1)S(1)} %bitcast.658), kind=kOutput, calls=%fused_computation.44 | convolution fusion | flops 2434793472 | bytes 22282240 | tf_op jit(solution)/shard_map/dot_general | solution.py:332
  284.2 7.2 %convolution_convert_fusion = bf16[1024,2304]{1,0:T(8,128)(2,1)S(1)} fusion(bf16[512,2304]{1,0:T(8,128)(2,1)S(1)} %copy-done.84, bf16[512,2304]{1,0:T(8,128)(2,1)S(1)} %copy-done.79, bf16[512,1024]{1,0:T(8,128)(2,1)} %collective-permute-done.36, bf16[512,1024]{1,0:T(8,128)(2,1)} %broadcast_select_fusion.4), kind=kOutput, calls=%fused_computation.22 | convolution fusion | flops 4847828992 | bytes 11534336 | tf_op jit(solution)/shard_map/dot_general | solution.py:82
  294.4 6.0 convolution_convert_fusion.2
  300.5 13.8 %collective-permute-done.37 = bf16[512,1024]{1,0:T(8,128)(2,1)S(1)} collective-permute-done((bf16[512,1024]{1,0:T(8,128)(2,1)S(1)}, bf16[512,1024]{1,0:T(8,128)(2,1)S(1)}, u32[]{:S(2)}, u32[]{:S(2)}) %collective-permute-start.37) | collective-permute-done | bytes 1048608 | tf_op jit(solution)/shard_map/ppermute | solution.py:176
  322.3 20.0 %collective-permute-done.38 = bf16[512,1024]{1,0:T(8,128)(2,1)S(1)} collective-permute-done((bf16[512,1024]{1,0:T(8,128)(2,1)S(1)}, bf16[512,1024]{1,0:T(8,128)(2,1)S(1)}, u32[]{:S(2)}, u32[]{:S(2)}) %collective-permute-start.38) | collective-permute-done | bytes 1048608 | tf_op jit(solution)/shard_map/ppermute | solution.py:176
  348.4 5.9 fusion.81
  376.5 14.4 %fusion.2 = (f32[4,2,512]{2,1,0:T(2,128)S(1)}, f32[4,1024,512,2]{2,1,3,0:T(8,128)}) fusion(f32[4,2,512,1024]{2,3,1,0:T(8,128)} %get-tuple-element.164, f32[4,2,512]{2,1,0:T(2,128)S(1)} %copy-done.59, bf16[1024,4,64,1]{0,2,3,1:T(8,128)(2,1)} %bitcast.694, bf16[512,4,2,64]{0,3,2,1:T(8,128)(2,1)} %bitcast.685), kind=kOutput, calls=%fused_computation.4 | convolution fusion | flops 549449728 | bytes 34635776 | tf_op jit(solution)/shard_map/qgrd,kgd->grqk/dot_general | solution.py:393
  390.8 9.2 %fusion.78 = bf16[1024,4,64]{0,2,1:T(8,128)(2,1)} fusion(bf16[512,4,2,64]{0,3,2,1:T(8,128)(2,1)S(1)} %bitcast.686, f32[512,4,64]{0,2,1:T(8,128)S(1)} %copy-done.85, f32[4,2,512,1024]{2,3,1,0:T(8,128)} %get-tuple-element.164, f32[4,2,512]{2,1,0:T(2,128)S(1)} %copy-done.59), kind=kOutput, calls=%fused_computation.165 | convolution fusion | flops 545783808 | bytes 18366464 | tf_op jit(solution)/shard_map/grqk,qgrd->kgd/dot_general | solution.py:420
  400.1 12.3 %fusion.4 = bf16[4,2,512,1024]{2,3,1,0:T(8,128)(2,1)S(1)} fusion(f32[4,1024,512,2]{2,1,3,0:T(8,128)} %get-tuple-element.170, f32[4,2,512]{2,1,0:T(2,128)S(1)} %get-tuple-element.169, f32[4,2,512,1024]{2,3,1,0:T(8,128)} %get-tuple-element.164, f32[4,2,512]{2,1,0:T(2,128)S(1)} %copy-done.59), kind=kLoop, calls=%fused_computation.6 | loop fusion | flops 16777216 | bytes 41975808 | tf_op jit(solution)/shard_map/convert_element_type | solution.py:400
  515.0 7.4 %fusion.42 = (f32[512,1024]{1,0:T(8,128)}, bf16[512,1024]{1,0:T(8,128)(2,1)}) fusion(bf16[512,1024]{1,0:T(8,128)(2,1)S(1)} %copy-done.4, f32[512,1024]{1,0:T(8,128)S(1)} %get-tuple-element.173, f32[512]{0:T(512)S(1)} %broadcast_multiply_fusion.2, f32[1024]{0:T(1024)S(1)} %copy-done.56, f32[512]{0:T(512)S(1)} %copy-done.62, ...), kind=kOutput, calls=%fused_computation.101 | convolution fusion | flops 2426404864 | bytes 19677184 | tf_op jit(solution)/shard_map/dot_general | solution.py:88
  575.0 9.0 %collective-permute-done.50 = bf16[64,1536]{1,0:T(8,128)(2,1)S(1)} collective-permute-done((bf16[64,1536]{1,0:T(8,128)(2,1)S(1)}, bf16[64,1536]{1,0:T(8,128)(2,1)S(1)}, u32[]{:S(2)}, u32[]{:S(2)}) %collective-permute-start.50) | collective-permute-done | bytes 196640 | tf_op jit(solution)/shard_map/ppermute | solution.py:168
  (536 shorter events, 386.0 us)
Async XLA Ops:
  3.3 30.5 %collective-permute-start.2 = (bf16[64,1664]{1,0:T(8,128)(2,1)S(1)}, bf16[64,1664]{1,0:T(8,128)(2,1)}, u32[]{:S(2)}, u32[]{:S(2)}) collective-permute-start(bf16[64,1664]{1,0:T(8,128)(2,1)S(1)} %concatenate.81), channel_id=1, source_target_pairs={{8,0},{10,2},{16,8},{18,10},{24,16},{26,18},{28,24},{30,26},{20,28... | collective-permute-start | bytes 638984 | tf_op jit(solution)/shard_map/ppermute | solution.py:133
  6.4 48.9 %collective-permute-start.26 = (bf16[64,2304]{1,0:T(8,128)(2,1)}, bf16[64,2304]{1,0:T(8,128)(2,1)}, u32[]{:S(2)}, u32[]{:S(2)}) collective-permute-start(bf16[64,2304]{1,0:T(8,128)(2,1)} %bitcast.689), channel_id=1, source_target_pairs={{0,8},{2,10},{8,16},{10,18},{16,24},{18,26},{24,28},{26,30},{28,20... | collective-permute-start | bytes 884744 | tf_op jit(solution)/shard_map/ppermute | solution.py:128
  8.4 49.2 %collective-permute-start.27 = (bf16[64,2304]{1,0:T(8,128)(2,1)}, bf16[64,2304]{1,0:T(8,128)(2,1)}, u32[]{:S(2)}, u32[]{:S(2)}) collective-permute-start(bf16[64,2304]{1,0:T(8,128)(2,1)} %bitcast.690), channel_id=1, source_target_pairs={{8,0},{10,2},{16,8},{18,10},{24,16},{26,18},{28,24},{30,26},{20,28... | collective-permute-start | bytes 884744 | tf_op jit(solution)/shard_map/ppermute | solution.py:133
  8.5 53.6 %collective-permute-start.11 = (bf16[64,2304]{1,0:T(8,128)(2,1)}, bf16[64,2304]{1,0:T(8,128)(2,1)}, u32[]{:S(2)}, u32[]{:S(2)}) collective-permute-start(bf16[64,2304]{1,0:T(8,128)(2,1)} %param.36), channel_id=1, source_target_pairs={{8,0},{10,2},{16,8},{18,10},{24,16},{26,18},{28,24},{30,26},{20,28... | collective-permute-start | bytes 884744 | tf_op jit(solution)/shard_map/ppermute | solution.py:133
  32.7 28.1 %collective-permute-start.10 = (bf16[64,2304]{1,0:T(8,128)(2,1)S(1)}, bf16[64,2304]{1,0:T(8,128)(2,1)S(1)}, u32[]{:S(2)}, u32[]{:S(2)}) collective-permute-start(bf16[64,2304]{1,0:T(8,128)(2,1)S(1)} %copy-done.48), channel_id=1, source_target_pairs={{0,8},{2,10},{8,16},{10,18},{16,24},{18,26},{24,28},{26,30},{28,20... | collective-permute-start | bytes 884744 | tf_op jit(solution)/shard_map/ppermute | solution.py:128
  53.1 79.9 %collective-permute-start = (bf16[512,1024]{0,1:T(8,128)(2,1)S(1)}, bf16[512,1024]{0,1:T(8,128)(2,1)S(1)}, u32[]{:S(2)}, u32[]{:S(2)}) collective-permute-start(bf16[512,1024]{0,1:T(8,128)(2,1)S(1)} %copy-done.17), channel_id=1, source_target_pairs={{1,0},{0,1},{3,2},{2,3},{5,4},{4,5},{7,6},{6,7},{9,8},{8,9},{11,10... | collective-permute-start | bytes 3145736 | tf_op jit(solution)/shard_map/ppermute | solution.py:176
  55.3 160.5 %collective-permute-start.36 = (bf16[512,1024]{1,0:T(8,128)(2,1)}, bf16[512,1024]{1,0:T(8,128)(2,1)}, u32[]{:S(2)}, u32[]{:S(2)}) collective-permute-start(bf16[512,1024]{1,0:T(8,128)(2,1)} %broadcast_select_fusion.4), channel_id=1, source_target_pairs={{1,0},{0,1},{3,2},{2,3},{5,4},{4,5},{7,6},{6,7},{9,8},{8,9},{11,10... | collective-permute-start | bytes 3145736 | tf_op jit(solution)/shard_map/ppermute | solution.py:176
  62.1 27.6 %collective-permute-start.28 = (bf16[64,2304]{1,0:T(8,128)(2,1)}, bf16[64,2304]{1,0:T(8,128)(2,1)S(1)}, u32[]{:S(2)}, u32[]{:S(2)}) collective-permute-start(bf16[64,2304]{1,0:T(8,128)(2,1)} %collective-permute-done.26), channel_id=1, source_target_pairs={{0,8},{2,10},{8,16},{10,18},{16,24},{18,26},{24,28},{26,30},{28,20... | collective-permute-start | bytes 884744 | tf_op jit(solution)/shard_map/ppermute | solution.py:128
  146.0 60.6 %collective-permute-start.17 = (bf16[8,64,2304]{2,1,0:T(8,128)(2,1)}, bf16[8,64,2304]{2,1,0:T(8,128)(2,1)}, u32[]{:S(2)}, u32[]{:S(2)}) collective-permute-start(bf16[8,64,2304]{2,1,0:T(8,128)(2,1)} %bitcast_dynamic-update-slice_fusion.16), channel_id=1, source_target_pairs={{0,2},{2,0},{4,6},{6,4},{8,10},{10,8},{12,14},{14,12},{16,18},{18,... | collective-permute-start | bytes 7077896 | tf_op jit(solution)/shard_map/ppermute | solution.py:137
  146.8 51.0 %collective-permute-start.33 = (bf16[8,64,2304]{2,1,0:T(8,128)(2,1)}, bf16[8,64,2304]{2,1,0:T(8,128)(2,1)}, u32[]{:S(2)}, u32[]{:S(2)}) collective-permute-start(bf16[8,64,2304]{2,1,0:T(8,128)(2,1)} %bitcast_dynamic-update-slice_fusion.1), channel_id=1, source_target_pairs={{0,2},{2,0},{4,6},{6,4},{8,10},{10,8},{12,14},{14,12},{16,18},{18,... | collective-permute-start | bytes 7077896 | tf_op jit(solution)/shard_map/ppermute | solution.py:137
  148.0 53.4 %collective-permute-start.25 = (bf16[8,64,2304]{2,1,0:T(8,128)(2,1)}, bf16[8,64,2304]{2,1,0:T(8,128)(2,1)}, u32[]{:S(2)}, u32[]{:S(2)}) collective-permute-start(bf16[8,64,2304]{2,1,0:T(8,128)(2,1)} %bitcast_dynamic-update-slice_fusion.8), channel_id=1, source_target_pairs={{0,2},{2,0},{4,6},{6,4},{8,10},{10,8},{12,14},{14,12},{16,18},{18,... | collective-permute-start | bytes 7077896 | tf_op jit(solution)/shard_map/ppermute | solution.py:137
  267.1 242.8 %collective-permute-start.35 = (bf16[512,1024]{1,0:T(8,128)(2,1)}, bf16[512,1024]{1,0:T(8,128)(2,1)}, u32[]{:S(2)}, u32[]{:S(2)}) collective-permute-start(bf16[512,1024]{1,0:T(8,128)(2,1)} %convolution_convert_fusion.5), channel_id=1, source_target_pairs={{1,0},{0,1},{3,2},{2,3},{5,4},{4,5},{7,6},{6,7},{9,8},{8,9},{11,10... | collective-permute-start | bytes 3145736 | tf_op jit(solution)/shard_map/ppermute | solution.py:176
  273.2 41.1 %collective-permute-start.37 = (bf16[512,1024]{1,0:T(8,128)(2,1)S(1)}, bf16[512,1024]{1,0:T(8,128)(2,1)S(1)}, u32[]{:S(2)}, u32[]{:S(2)}) collective-permute-start(bf16[512,1024]{1,0:T(8,128)(2,1)S(1)} %add_convert_fusion.1), channel_id=1, source_target_pairs={{1,0},{0,1},{3,2},{2,3},{5,4},{4,5},{7,6},{6,7},{9,8},{8,9},{11,10... | collective-permute-start | bytes 3145736 | tf_op jit(solution)/shard_map/ppermute | solution.py:176
  293.9 156.4 %collective-permute-start.74 = (bf16[8,64,2304]{2,1,0:T(8,128)(2,1)}, bf16[8,64,2304]{2,1,0:T(8,128)(2,1)}, u32[]{:S(2)}, u32[]{:S(2)}) collective-permute-start(bf16[8,64,2304]{2,1,0:T(8,128)(2,1)} %get-tuple-element.97), channel_id=1, source_target_pairs={{0,2},{2,0},{4,6},{6,4},{8,10},{10,8},{12,14},{14,12},{16,18},{18,... | collective-permute-start | bytes 7077896 | tf_op jit(solution)/shard_map/ppermute | solution.py:153
  293.9 160.0 %collective-permute-start.66 = (bf16[8,64,2304]{2,1,0:T(8,128)(2,1)}, bf16[8,64,2304]{2,1,0:T(8,128)(2,1)}, u32[]{:S(2)}, u32[]{:S(2)}) collective-permute-start(bf16[8,64,2304]{2,1,0:T(8,128)(2,1)} %get-tuple-element.103), channel_id=1, source_target_pairs={{0,2},{2,0},{4,6},{6,4},{8,10},{10,8},{12,14},{14,12},{16,18},{18,... | collective-permute-start | bytes 7077896 | tf_op jit(solution)/shard_map/ppermute | solution.py:153
  321.6 135.6 %collective-permute-start.58 = (bf16[8,64,2304]{2,1,0:T(8,128)(2,1)}, bf16[8,64,2304]{2,1,0:T(8,128)(2,1)}, u32[]{:S(2)}, u32[]{:S(2)}) collective-permute-start(bf16[8,64,2304]{2,1,0:T(8,128)(2,1)} %get-tuple-element.109), channel_id=1, source_target_pairs={{0,2},{2,0},{4,6},{6,4},{8,10},{10,8},{12,14},{14,12},{16,18},{18,... | collective-permute-start | bytes 7077896 | tf_op jit(solution)/shard_map/ppermute | solution.py:153
  449.1 94.9 %collective-permute-start.45 = (bf16[8,64,1536]{2,1,0:T(8,128)(2,1)}, bf16[8,64,1536]{2,1,0:T(8,128)(2,1)}, u32[]{:S(2)}, u32[]{:S(2)}) collective-permute-start(bf16[8,64,1536]{2,1,0:T(8,128)(2,1)} %get-tuple-element.125), channel_id=1, source_target_pairs={{0,2},{2,0},{4,6},{6,4},{8,10},{10,8},{12,14},{14,12},{16,18},{18,... | collective-permute-start | bytes 4718600 | tf_op jit(solution)/shard_map/ppermute | solution.py:153
  450.3 31.7 %collective-permute-start.39 = (bf16[512,1024]{1,0:T(8,128)(2,1)S(1)}, bf16[512,1024]{1,0:T(8,128)(2,1)S(1)}, u32[]{:S(2)}, u32[]{:S(2)}) collective-permute-start(bf16[512,1024]{1,0:T(8,128)(2,1)S(1)} %add_convert_fusion), channel_id=1, source_target_pairs={{1,0},{0,1},{3,2},{2,3},{5,4},{4,5},{7,6},{6,7},{9,8},{8,9},{11,10... | collective-permute-start | bytes 3145736 | tf_op jit(solution)/shard_map/ppermute | solution.py:176
  457.1 65.9 %collective-permute-start.79 = (bf16[64,2304]{1,0:T(8,128)(2,1)}, bf16[64,2304]{1,0:T(8,128)(2,1)}, u32[]{:S(2)}, u32[]{:S(2)}) collective-permute-start(bf16[64,2304]{1,0:T(8,128)(2,1)} %get-tuple-element.95), channel_id=1, source_target_pairs={{8,0},{10,2},{16,8},{18,10},{24,16},{26,18},{28,24},{30,26},{20,28... | collective-permute-start | bytes 884744 | tf_op jit(solution)/shard_map/ppermute | solution.py:168
  499.0 32.5 %collective-permute-start.63 = (bf16[64,2304]{1,0:T(8,128)(2,1)S(1)}, bf16[64,2304]{1,0:T(8,128)(2,1)S(1)}, u32[]{:S(2)}, u32[]{:S(2)}) collective-permute-start(bf16[64,2304]{1,0:T(8,128)(2,1)S(1)} %get-tuple-element.107), channel_id=1, source_target_pairs={{8,0},{10,2},{16,8},{18,10},{24,16},{26,18},{28,24},{30,26},{20,28... | collective-permute-start | bytes 884744 | tf_op jit(solution)/shard_map/ppermute | solution.py:168
  522.4 63.2 %collective-permute-start.69 = (bf16[64,2304]{1,0:T(8,128)(2,1)S(1)}, bf16[64,2304]{1,0:T(8,128)(2,1)S(1)}, u32[]{:S(2)}, u32[]{:S(2)}) collective-permute-start(bf16[64,2304]{1,0:T(8,128)(2,1)S(1)} %get-tuple-element.98), channel_id=1, source_target_pairs={{0,8},{2,10},{8,16},{10,18},{16,24},{18,26},{24,28},{26,30},{28,20... | collective-permute-start | bytes 884744 | tf_op jit(solution)/shard_map/ppermute | solution.py:168
  529.9 36.3 %collective-permute-start.78 = (bf16[64,2304]{1,0:T(8,128)(2,1)S(1)}, bf16[64,2304]{1,0:T(8,128)(2,1)S(1)}, u32[]{:S(2)}, u32[]{:S(2)}) collective-permute-start(bf16[64,2304]{1,0:T(8,128)(2,1)S(1)} %get-tuple-element.92), channel_id=1, source_target_pairs={{0,8},{2,10},{8,16},{10,18},{16,24},{18,26},{24,28},{26,30},{28,20... | collective-permute-start | bytes 884744 | tf_op jit(solution)/shard_map/ppermute | solution.py:168
  541.4 51.3 %collective-permute-start.62 = (bf16[64,2304]{1,0:T(8,128)(2,1)S(1)}, bf16[64,2304]{1,0:T(8,128)(2,1)S(1)}, u32[]{:S(2)}, u32[]{:S(2)}) collective-permute-start(bf16[64,2304]{1,0:T(8,128)(2,1)S(1)} %get-tuple-element.104), channel_id=1, source_target_pairs={{0,8},{2,10},{8,16},{10,18},{16,24},{18,26},{24,28},{26,30},{28,20... | collective-permute-start | bytes 884744 | tf_op jit(solution)/shard_map/ppermute | solution.py:168
  566.2 26.5 %collective-permute-start.65 = (bf16[64,2304]{1,0:T(8,128)(2,1)S(1)}, bf16[64,2304]{1,0:T(8,128)(2,1)S(1)}, u32[]{:S(2)}, u32[]{:S(2)}) collective-permute-start(bf16[64,2304]{1,0:T(8,128)(2,1)S(1)} %fusion.158), channel_id=1, source_target_pairs={{8,0},{10,2},{16,8},{18,10},{24,16},{26,18},{28,24},{30,26},{20,28... | collective-permute-start | bytes 884744 | tf_op jit(solution)/shard_map/ppermute | solution.py:168
  (152 other events, 1704.4 us)

commit v2 on v1

--- a/solution.py
+++ b/solution.py
@@ -113,6 +113,10 @@
     return (chips - 1 - longer, longer) if flip else (longer, chips - 1 - longer)
 
 
+def tie(*values):
+    return lax.optimization_barrier(values)
+
+
 def ring_gather(block, flip):
     chips = lax.axis_size("dp") // 2
     right, left, sibling = ring_perms(chips)
@@ -120,55 +124,120 @@
     core = index % 2
     place = ring_pos(index // 2, chips)
     count_right, count_left = hops(chips, flip)
-    lane = jnp.zeros((chips,) + block.shape, block.dtype)
-    lane = lax.dynamic_update_index_in_dim(lane, block, index // 2, 0)
+    steps = max(count_right, count_left)
+    whole = jnp.zeros((chips, 2) + block.shape, block.dtype)
+
+    def put(whole, value, pos, side):
+        return lax.dynamic_update_slice(
+            whole, value[None, None], (ring_chip(pos, chips), side, 0, 0)
+        )
+
+    whole = put(whole, block, place, core)
+    held, places = [block], [place]
     from_left, from_right = block, block
-    for step in range(1, max(count_right, count_left) + 1):
+    for step in range(1, steps + 1):
+        arrived = []
         if step <= count_right:
             from_left = lax.ppermute(from_left, "dp", right)
-            lane = lax.dynamic_update_index_in_dim(
-                lane, from_left, ring_chip(place - step, chips), 0
-            )
+            arrived.append((from_left, place - step))
         if step <= count_left:
             from_right = lax.ppermute(from_right, "dp", left)
-            lane = lax.dynamic_update_index_in_dim(
-                lane, from_right, ring_chip(place + step, chips), 0
-            )
-    other = lax.ppermute(lane, "dp", sibling)
-    first = jnp.where(core == 0, lane, other)
-    second = jnp.where(core == 0, other, lane)
-    return jnp.stack([first, second], axis=1).reshape(2 * chips * block.shape[0], -1)
-
-
-def ring_scatter(full, flip):
+            arrived.append((from_right, place + step))
+        proceed = yield [value for value, _ in arrived]
+        if proceed is not None:
+            arrived = [(value, pos) for value, (_, pos) in zip(proceed, arrived)]
+            if step <= count_right:
+                from_left = proceed[0]
+            if step <= count_left:
+                from_right = proceed[-1]
+        for value, pos in arrived:
+            whole = put(whole, value, pos, core)
+            held.append(value)
+            places.append(pos)
+        if step == (steps + 1) // 2 or step == steps:
+            other = lax.ppermute(jnp.stack(held), "dp", sibling)
+            for number, pos in enumerate(places):
+                whole = put(whole, other[number], pos, 1 - core)
+            held, places = [], []
+    return whole.reshape(2 * chips * block.shape[0], block.shape[1])
+
+
+def ring_scatter(arrays, flip):
     chips = lax.axis_size("dp") // 2
     right, left, sibling = ring_perms(chips)
     index = lax.axis_index("dp")
     core = index % 2
     place = ring_pos(index // 2, chips)
     count_right, count_left = hops(chips, flip)
-    pairs = full.reshape(chips, 2, full.shape[0] // (2 * chips), full.shape[1])
-    mine = jnp.where(core == 0, pairs[:, 0], pairs[:, 1])
-    theirs = jnp.where(core == 0, pairs[:, 1], pairs[:, 0])
+    pairs = [v.reshape(chips, 2, v.shape[0] // (2 * chips), v.shape[1]) for v in arrays]
+    theirs = jnp.concatenate(
+        [lax.dynamic_index_in_dim(v, 1 - core, 1, keepdims=False) for v in pairs], axis=2
+    )
     got = lax.ppermute(theirs, "dp", sibling)
 
     def chunk(pos):
         chip = ring_chip(pos, chips)
-        return lax.dynamic_index_in_dim(mine, chip, 0, keepdims=False).astype(
-            jnp.float32
-        ) + lax.dynamic_index_in_dim(got, chip, 0, keepdims=False).astype(jnp.float32)
-
+        own = jnp.concatenate(
+            [
+                lax.dynamic_slice(v, (chip, core, 0, 0), (1, 1) + v.shape[2:])[0, 0]
+                for v in pairs
+            ],
+            axis=1,
+        )
+        return own.astype(jnp.float32) + lax.dynamic_index_in_dim(
+            got, chip, 0, keepdims=False
+        ).astype(jnp.float32)
+
+    from_left, from_right = None, None
+    for step in range(max(count_right, count_left), 0, -1):
+        sends = []
+        if step <= count_right:
+            part = chunk(place + step)
+            if from_left is not None:
+                part = part + from_left.astype(jnp.float32)
+            sends.append(part.astype(jnp.bfloat16))
+        if step <= count_left:
+            part = chunk(place - step)
+            if from_right is not None:
+                part = part + from_right.astype(jnp.float32)
+            sends.append(part.astype(jnp.bfloat16))
+        proceed = yield sends
+        if proceed is not None:
+            sends = proceed
+        if step <= count_right:
+            from_left = lax.ppermute(sends[0], "dp", right)
+        if step <= count_left:
+            from_right = lax.ppermute(sends[-1], "dp", left)
     total = chunk(place)
-    for count, perm, sign in ((count_right, right, 1), (count_left, left, -1)):
-        received = None
-        for step in range(count, 0, -1):
-            partial = chunk(place + sign * step)
-            if received is not None:
-                partial = partial + received.astype(jnp.float32)
-            received = lax.ppermute(partial.astype(jnp.bfloat16), "dp", perm)
-        if received is not None:
-            total = total + received.astype(jnp.float32)
+    for part in (from_left, from_right):
+        if part is not None:
+            total = total + part.astype(jnp.float32)
     return total
+
+
+class Steps:
+    def __init__(self, ring):
+        self.ring = ring
+        self.waiting = next(ring)
+        self.result = None
+
+    def advance(self, value):
+        if self.waiting is None:
+            return value
+        value, *values = tie(value, *self.waiting)
+        try:
+            self.waiting = self.ring.send(values)
+        except StopIteration as end:
+            self.waiting, self.result = None, end.value
+        return value
+
+    def finish(self):
+        while self.waiting is not None:
+            try:
+                self.waiting = self.ring.send(None)
+            except StopIteration as end:
+                self.waiting, self.result = None, end.value
+        return self.result
 
 
 def shifted(values, shift):
@@ -256,12 +325,16 @@
         ],
         axis=1,
     )
-    attn_pack = ring_gather(
-        jnp.concatenate([w_query, key_weight, value_weight, w_out.T, gain_columns], axis=1), False
-    )
-    wg_all = ring_gather(w_gate, True)
-    wu_all = ring_gather(w_up, False)
-    wdt_all = ring_gather(w_down.T, True)
+    attn_pack = Steps(
+        ring_gather(
+            jnp.concatenate([w_query, key_weight, value_weight, w_out.T, gain_columns], axis=1),
+            False,
+        )
+    ).finish()
+    ffn_block = jnp.concatenate([w_gate, w_up, w_down.T], axis=1)
+    attn_pack, ffn_block = tie(attn_pack, ffn_block)
+    ffn_ring = Steps(ring_gather(ffn_block, True))
+    fw = w_gate.shape[1]
     wq_all = attn_pack[:, :qw]
     wk_all = attn_pack[:, qw : qw + kw]
     wv_all = attn_pack[:, qw + kw : qw + 2 * kw]
@@ -289,6 +362,7 @@
     key_normed, key_inv = rows_normalize(key_unrotated, kgain_wide)
     query_low = apply_rotary(query_normed, cosine_table, sine_table).astype(jnp.bfloat16)
     key_low = apply_rotary(key_normed, cosine_table, sine_table).astype(jnp.bfloat16)
+    query_low = ffn_ring.advance(query_low)
     query_grouped = query_low.reshape(group_rows, kv_heads, repeat, head_dim)
     outputs = []
     kept_stats = []
@@ -319,6 +393,7 @@
             )
         )
         kept_stats.append((row_peak, row_total))
+        outputs[-1] = ffn_ring.advance(outputs[-1])
     heads_low = (
         jnp.concatenate(outputs, axis=0)
         .reshape(group_rows, query_heads * head_dim)
@@ -326,6 +401,8 @@
     )
     mixed = tokens_wide + scatter_parts(lambda k: contract_cols(part_of(heads_low, k), wot_all))
     ffn_in, ffn_inv = rows_normalize(mixed, ffn_gain_all.astype(jnp.float32))
+    ffn_pack = ffn_ring.finish()
+    wg_all, wu_all, wdt_all = ffn_pack[:, :fw], ffn_pack[:, fw : 2 * fw], ffn_pack[:, 2 * fw :]
     ffn_parts = gather_parts(ffn_in.astype(jnp.bfloat16))
     gates, ups, hiddens, grad_gates, grad_ups = [], [], [], [], []
     for ffn_rows, grad_rows in zip(ffn_parts, grad_parts):
@@ -352,16 +429,15 @@
     output = result.astype(jnp.bfloat16)
     ffn_cat = jnp.concatenate(ffn_parts, axis=0)
     grad_cat = jnp.concatenate(grad_parts, axis=0)
-    ffn_sums = (
+    ffn_sum_ring = Steps(
         ring_scatter(
-            contract_rows(ffn_cat, jnp.concatenate(grad_gates, axis=0)).astype(jnp.bfloat16), False
-        ),
-        ring_scatter(
-            contract_rows(ffn_cat, jnp.concatenate(grad_ups, axis=0)).astype(jnp.bfloat16), True
-        ),
-        ring_scatter(
-            contract_rows(grad_cat, jnp.concatenate(hiddens, axis=0)).astype(jnp.bfloat16), False
-        ).T,
+            [
+                contract_rows(ffn_cat, jnp.concatenate(grad_gates, axis=0)).astype(jnp.bfloat16),
+                contract_rows(ffn_cat, jnp.concatenate(grad_ups, axis=0)).astype(jnp.bfloat16),
+                contract_rows(grad_cat, jnp.concatenate(hiddens, axis=0)).astype(jnp.bfloat16),
+            ],
+            False,
+        )
     )
     grad_heads = to_slots(
         [
@@ -377,6 +453,7 @@
         low_row = number * blk_rows
         high_row = low_row + blk_rows
         row_peak, row_total = kept_stats[number]
+        row_peak = ffn_sum_ring.advance(row_peak)
         allowed = block_mask(segment_index, valid_mask, low_row, high_row, high_row)
         scores = (
             jnp.einsum(
@@ -398,6 +475,7 @@
         )
         inner_sum = jnp.sum(probs_wide * grad_probs, axis=-1, keepdims=True)
         grad_scores = (probs_wide * (grad_probs - inner_sum)).astype(jnp.bfloat16)
+        grad_scores = ffn_sum_ring.advance(grad_scores)
         grad_query_parts.append(
             jnp.einsum(
                 "grqk,kgd->qgrd",
@@ -448,9 +526,13 @@
         tokens_wide, attn_inv, attn_gain_all.astype(jnp.float32), grad_attn_in
     )
     input_grad = grad_mixed + back_tokens
-    attn_pack_sum = ring_scatter(
-        jnp.concatenate([grad_wq, grad_wk, grad_wv, grad_wot], axis=1).astype(jnp.bfloat16), True
-    )
+    ffn_sum = ffn_sum_ring.finish()
+    ffn_sums = (ffn_sum[:, :fw], ffn_sum[:, fw : 2 * fw], ffn_sum[:, 2 * fw :].T)
+    attn_pack_sum = Steps(
+        ring_scatter(
+            [v.astype(jnp.bfloat16) for v in (grad_wq, grad_wk, grad_wv, grad_wot)], True
+        )
+    ).finish()
     attn_sums = (
         attn_pack_sum[:, :qw],
         attn_pack_sum[:, qw : qw + kw],

time: 608 us -> 531 us (0.87)
  waiting for transfers between devices: 186 us -> 124 us
  other arithmetic: 101 us -> 65.4 us
  starting transfers between devices: 80.4 us -> 56 us
  local copies, waits for them, and re-layouts: 56.1 us -> 79.4 us
  matrix products: 175 us -> 194 us
    ppermute x32 -> x18, waiting for transfers between devices: 67.6 us -> 33.4 us  [the longest x7 17.6 us: ring_scatter(): from_left = lax.ppermute(sends[0], 'dp', right)]
    ppermute x14 -> x7, waiting for transfers between devices: 45.7 us -> 24.4 us  [ring_gather(): from_left = lax.ppermute(from_left, 'dp', right)]
    convert_element_type x23 -> x10, other arithmetic: 38.8 us -> 19.3 us  [ring_scatter(): sends.append(part.astype(jnp.bfloat16))]
    sub x2, matrix products: 18.9 us -> 36.5 us  [per_device(): grad_scores = (probs_wide * (grad_probs - inner_sum)).astype(jnp.bfloat16)]
    ppermute x14 -> x7, starting transfers between devices: 18.8 us -> 2.49 us  [ring_gather(): from_right = lax.ppermute(from_right, 'dp', left)]
    unnamed x189 -> x274, local copies, waits for them, and re-layouts: 5.88 us -> 21 us
    another operation x11 -> x5, other arithmetic: 14 us -> 1.69 us  [the longest x8 11.7 us: ring_gather(): jnp.stack([first, second], axis=1).reshape(2 * chips * block.shape[0], -1)]
    reduce_sum x0 -> x2, other arithmetic: none -> 11 us  [per_device(): row_total = jnp.sum(exp_terms, axis=-1, keepdims=True)]
  transfers between devices with their start and end apart: 82 -> 52, of which waited for: 39 -> 25; matrix products, arithmetic and copies ran while one was open for 50% -> 54% of each run, Pallas kernels for 0% -> 0%
where the time goes in v2:
time: 531 us; the launch traced here: 522 us
  matrix products  194 us (37%)
  waiting for transfers between devices  124 us (23%)
  local copies, waits for them, and re-layouts  79.4 us (15%)
  other arithmetic  65.4 us (12%)
  starting transfers between devices  56 us (11%)
    ppermute x8, waiting for transfers between devices, shifted(): lax.ppermute(values, 'tensor', [((i + shift) % size, i) for i in range(si...  41.6 us
    dot_general x14, matrix products, contract_cols(): lax.dot_general(left, right, (((1,), (1,)), ((), ())), preferred_element_...  41.5 us
    sub x2, matrix products, per_device(): grad_scores = (probs_wide * (grad_probs - inner_sum)).astype(jnp.bfloat16)  36.5 us
    dot_general x7, matrix products, contract_rows(): lax.dot_general(left, right, (((0,), (0,)), ((), ())), preferred_element_...  28.5 us
    dynamic_update_slice x32, local copies, waits for them, and re-layouts, put(): lax.dynamic_update_slice(whole, value[None, None], (ring_chip(pos, chips)...  25 us
    ppermute x7, waiting for transfers between devices, ring_gather(): from_left = lax.ppermute(from_left, 'dp', right)  24.4 us
    unnamed x274, local copies, waits for them, and re-layouts  21 us
    ppermute x7, waiting for transfers between devices, ring_gather(): from_right = lax.ppermute(from_right, 'dp', left)  19.8 us
  transfers between devices with their start and end apart: 52, of which 25 were waited for; matrix products, arithmetic and copies ran while one was open for 54% of the time, Pallas kernels for 0%

profile of v2, /device:TPU:0, one launch (start us, length us, event | category | flops | bytes accessed | tf_op | source)
XLA Modules:
  0.0 522.5 jit_solution(14042761040740479884)
XLA Ops:
  36.7 5.7 %collective-permute-done.6 = bf16[64,1664]{1,0:T(8,128)(2,1)S(1)} collective-permute-done((bf16[64,1664]{1,0:T(8,128)(2,1)S(1)}, bf16[64,1664]{1,0:T(8,128)(2,1)S(1)}, u32[]{:S(2)}, u32[]{:S(2)}) %collective-permute-start.6) | collective-permute-done | bytes 213024 | tf_op jit(solution)/shard_map/ppermute | solution.py:141
  65.0 6.4 %broadcast_in_dim.208 = bf16[8,2,64,6912]{3,2,1,0:T(8,128)(2,1)} broadcast(bf16[]{:T(256)} %constant.445.clone.1), dimensions={} | broadcast | bytes 14155778 | tf_op jit(solution)/shard_map/broadcast_in_dim | solution.py:128
  92.2 7.3 %fusion.5 = (f32[4,2,512]{2,1,0:T(2,128)S(1)}, f32[4,1024,512,2]{2,1,3,0:T(8,128)}) fusion(pred[512,1024]{0,1:T(8,128)(4,1)S(1)} %copy-done.39, bf16[512,4,2,64]{0,3,2,1:T(8,128)(2,1)S(1)} %bitcast.596, bf16[1024,4,32]{0,2,1:T(8,128)(2,1)S(1)} %get-tuple-element.183, bf16[1024,4,32]{0,2,1:T(8,128)(2,1)S(1)} %get-tuple-element.182), kind=kOutput, calls=%fused_computation.11 | convolution fusion | flops 550498304 | bytes 18366464 | tf_op jit(solution)/shard_map/qgrd,kgd->grqk/dot_general | solution.py:374
  99.5 9.2 %fusion.4 = f32[4,2,512]{2,1,0:T(2,128)S(1)} fusion(f32[4,1024,512,2]{2,1,3,0:T(8,128)} %get-tuple-element.240, f32[4,2,512]{2,1,0:T(2,128)S(1)} %get-tuple-element.239, pred[512,1024]{0,1:T(8,128)(4,1)} %fusion.77), kind=kLoop, calls=%fused_computation.10 | loop fusion | flops 16773120 | bytes 17334272 | tf_op jit(solution)/shard_map/reduce_sum | solution.py:385
  108.8 8.3 %fusion.104 = bf16[512,4,2,64]{0,3,2,1:T(8,128)(2,1)S(1)} fusion(bf16[1024,4,64,1]{0,2,3,1:T(8,128)(2,1)} %bitcast.622, f32[4,1024,512,2]{2,1,3,0:T(8,128)} %get-tuple-element.240, f32[4,2,512]{2,1,0:T(2,128)S(1)} %fusion.4, f32[4,2,512]{2,1,0:T(2,128)S(1)} %get-tuple-element.239, pred[512,1024]{0,1:T(8,128)(4,1)} %fusion.77), kind=kOutput, calls=%fused_computation.176 | convolution fusion | flops 557842432 | bytes 18382848 | tf_op jit(solution)/shard_map/grqk,kgd->qgrd/dot_general | solution.py:388
  133.4 11.7 %collective-permute-done.14 = bf16[64,6912]{1,0:T(8,128)(2,1)S(1)} collective-permute-done((bf16[64,6912]{1,0:T(8,128)(2,1)}, bf16[64,6912]{1,0:T(8,128)(2,1)S(1)}, u32[]{:S(2)}, u32[]{:S(2)}) %collective-permute-start.14) | collective-permute-done | bytes 884768 | tf_op jit(solution)/shard_map/ppermute | solution.py:141
  151.8 16.3 %collective-permute-done.18 = bf16[64,6912]{1,0:T(8,128)(2,1)S(1)} collective-permute-done((bf16[64,6912]{1,0:T(8,128)(2,1)S(1)}, bf16[64,6912]{1,0:T(8,128)(2,1)S(1)}, u32[]{:S(2)}, u32[]{:S(2)}) %collective-permute-start.18) | collective-permute-done | bytes 884768 | tf_op jit(solution)/shard_map/ppermute | solution.py:144
  199.7 6.7 %fusion.42 = f32[512,2304]{1,0:T(8,128)} fusion(bf16[512,1024]{1,0:T(8,128)(2,1)S(1)} %collective-permute-done.20, bf16[1024,6912]{1,0:T(8,128)(2,1)} %bitcast.76), kind=kOutput, calls=%fused_computation.83 | convolution fusion | flops 2415919104 | bytes 10485760 | tf_op jit(solution)/shard_map/dot_general | solution.py:410
  206.4 8.5 %multiply_convert_fusion.1 = (bf16[512,2304]{1,0:T(8,128)(2,1)S(1)}, bf16[512,2304]{1,0:T(8,128)(2,1)S(1)}, bf16[512,2304]{1,0:T(8,128)(2,1)}) fusion(f32[512,2304]{1,0:T(8,128)S(1)} %fusion.30, f32[512,2304]{1,0:T(8,128)} %fusion.42, bf16[512,1024]{1,0:T(8,128)(2,1)S(1)} %collective-permute-done.20, bf16[1024,6912]{1,0:T(8,128)(2,1)} %bitcast.76), kind=kOutput, calls=%fused_computation.46 | convolution fusion | flops 2434793472 | bytes 22282240 | tf_op jit(solution)/shard_map/dot_general | solution.py:409
  214.9 6.7 %fusion.101 = bf16[512,1024]{1,0:T(8,128)(2,1)S(1)} fusion(bf16[512,2304]{1,0:T(8,128)(2,1)S(1)} %get-tuple-element.133, bf16[1024,6912]{1,0:T(8,128)(2,1)} %bitcast.76), kind=kOutput, calls=%fused_computation.173 | convolution fusion | flops 2416443392 | bytes 8126464 | tf_op jit(solution)/shard_map/dot_general | solution.py:88
  222.2 7.6 %multiply_convert_fusion.3 = (bf16[512,2304]{1,0:T(8,128)(2,1)S(1)}, bf16[512,2304]{1,0:T(8,128)(2,1)S(1)}, bf16[512,2304]{1,0:T(8,128)(2,1)}) fusion(f32[512,2304]{1,0:T(8,128)S(1)} %fusion.32, f32[512,2304]{1,0:T(8,128)S(1)} %fusion.44, bf16[512,1024]{1,0:T(8,128)(2,1)S(1)} %multiply_convert_fusion.6, bf16[1024,6912]{1,0:T(8,128)(2,1)} %bitcast.76), kind=kOutput, calls=%fused_computation.48 | convolution fusion | flops 2434793472 | bytes 22282240 | tf_op jit(solution)/shard_map/dot_general | solution.py:409
  229.8 5.6 %convolution_convert_fusion.2 = bf16[1024,2304]{1,0:T(8,128)(2,1)S(1)} fusion(bf16[512,2304]{1,0:T(8,128)(2,1)S(1)} %get-tuple-element.132, bf16[512,2304]{1,0:T(8,128)(2,1)S(1)} %get-tuple-element.129, bf16[512,1024]{1,0:T(8,128)(2,1)S(1)} %collective-permute-done.20, bf16[512,1024]{1,0:T(8,128)(2,1)S(1)} %multiply_convert_fusion.6), kind=kOutput, calls=%fused_computation.28 | convolution fusion | flops 4847828992 | bytes 11534336 | tf_op jit(solution)/shard_map/dot_general | solution.py:82
  237.0 7.2 %convolution_convert_fusion = bf16[1024,2304]{1,0:T(8,128)(2,1)S(1)} fusion(bf16[512,2304]{1,0:T(8,128)(2,1)S(1)} %copy-done.132, bf16[512,2304]{1,0:T(8,128)(2,1)S(1)} %get-tuple-element.130, bf16[512,1024]{1,0:T(8,128)(2,1)} %collective-permute-done.22, bf16[512,1024]{1,0:T(8,128)(2,1)} %broadcast_select_fusion), kind=kOutput, calls=%fused_computation.26 | convolution fusion | flops 4847828992 | bytes 11534336 | tf_op jit(solution)/shard_map/dot_general | solution.py:82
  244.3 8.0 %convolution_convert_fusion.1 = bf16[1024,2304]{1,0:T(8,128)(2,1)S(1)} fusion(bf16[512,2304]{1,0:T(8,128)(2,1)} %get-tuple-element.134, bf16[512,2304]{1,0:T(8,128)(2,1)} %get-tuple-element.131, bf16[512,1024]{1,0:T(8,128)(2,1)S(1)} %collective-permute-done.20, bf16[512,1024]{1,0:T(8,128)(2,1)S(1)} %multiply_convert_fusion.6), kind=kOutput, calls=%fused_computation.27 | convolution fusion | flops 4847828992 | bytes 11534336 | tf_op jit(solution)/shard_map/dot_general | solution.py:82
  276.4 14.7 %collective-permute-done.23 = bf16[512,1024]{1,0:T(8,128)(2,1)S(1)} collective-permute-done((bf16[512,1024]{1,0:T(8,128)(2,1)S(1)}, bf16[512,1024]{1,0:T(8,128)(2,1)S(1)}, u32[]{:S(2)}, u32[]{:S(2)}) %collective-permute-start.23) | collective-permute-done | bytes 1048608 | tf_op jit(solution)/shard_map/ppermute | solution.py:245
  291.1 6.1 %multiply_reduce_fusion = (f32[1024]{0:T(1024)}, f32[512]{0:T(512)S(1)}, f32[512,1024]{1,0:T(8,128)S(1)}) fusion(f32[512,1024]{1,0:T(8,128)S(1)} %get-tuple-element.244, f32[512]{0:T(512)S(1)} %add_rsqrt_fusion.4, f32[1024]{0:T(1024)S(1)} %get-tuple-element.123, bf16[512,1024]{1,0:T(8,128)(2,1)S(1)} %collective-permute-done.23, ...), kind=kOutput, calls=%fused_computation.129 | convolution fusion | flops 2420636160 | bytes 14430208 | tf_op jit(solution)/shard_map/dot_general | solution.py:88
  300.3 5.9 %add_convert_fusion.2 = bf16[512,1024]{1,0:T(8,128)(2,1)} fusion(f32[512,1024]{1,0:T(8,128)S(1)} %get-tuple-element.244, bf16[512,1024]{1,0:T(8,128)(2,1)S(1)} %collective-permute-done.21, bf16[512,2304]{1,0:T(8,128)(2,1)S(1)} %copy-done.126, bf16[1024,6912]{1,0:T(8,128)(2,1)} %bitcast.76), kind=kOutput, calls=%fused_computation.137 | convolution fusion | flops 2418016256 | bytes 11272192 | tf_op jit(solution)/shard_map/dot_general | solution.py:88
  306.2 16.4 %collective-permute-done.25 = bf16[512,1024]{1,0:T(8,128)(2,1)S(1)} collective-permute-done((bf16[512,1024]{1,0:T(8,128)(2,1)S(1)}, bf16[512,1024]{1,0:T(8,128)(2,1)S(1)}, u32[]{:S(2)}, u32[]{:S(2)}) %collective-permute-start.25) | collective-permute-done | bytes 1048608 | tf_op jit(solution)/shard_map/ppermute | solution.py:245
  340.2 13.7 %fusion.7 = bf16[4,2,512,512]{2,3,1,0:T(8,128)(2,1)} fusion(bf16[512,4,64,1]{0,2,3,1:T(8,128)(2,1)} %bitcast.620, bf16[512,4,2,64]{0,3,2,1:T(8,128)(2,1)} %bitcast.617, f32[4,2,512]{2,1,0:T(2,128)} %copy-done.104, f32[4,2,512]{2,1,0:T(2,128)S(1)} %copy-done.96, f32[4,512,512,2]{2,1,3,0:T(8,128)} %copy-done, pred[512,512]{0,1:T(8,128)(4,1)} %fusion.134), kind=kOutput, calls=%fused_computation.15 | convolution fusion | flops 562041344 | bytes 13664256 | tf_op jit(solution)/shard_map/sub | solution.py:477
  373.6 7.6 %collective-permute-done.28 = bf16[64,6912]{1,0:T(8,128)(2,1)S(1)} collective-permute-done((bf16[64,6912]{1,0:T(8,128)(2,1)S(1)}, bf16[64,6912]{1,0:T(8,128)(2,1)S(1)}, u32[]{:S(2)}, u32[]{:S(2)}) %collective-permute-start.28) | collective-permute-done | bytes 884768 | tf_op jit(solution)/shard_map/ppermute | solution.py:210
  386.8 22.7 %fusion.3 = bf16[4,2,512,1024]{2,3,1,0:T(8,128)(2,1)} fusion(f32[4,2,512]{2,1,0:T(2,128)} %copy-done.109, f32[4,2,512]{2,1,0:T(2,128)S(1)} %copy-done.108, f32[4,1024,512,2]{2,1,3,0:T(8,128)} %get-tuple-element.240, pred[512,1024]{0,1:T(8,128)(4,1)} %fusion.77, bf16[1024,4,64,1]{0,2,3,1:T(8,128)(2,1)} %bitcast.623, bf16[512,4,2,64]{0,3,2,1:T(8,128)(2,1)} %bitcast.615), kind=kOutput, calls=%fused_computation.5 | convolution fusion | flops 1124078592 | bytes 26771456 | tf_op jit(solution)/shard_map/sub | solution.py:477
  409.6 9.0 %fusion.117 = bf16[1024,4,64]{0,2,1:T(8,128)(2,1)S(1)} fusion(bf16[512,4,2,64]{0,3,2,1:T(8,128)(2,1)} %bitcast.616, f32[512,4,64]{0,2,1:T(8,128)} %fusion.122, f32[4,1024,512,2]{2,1,3,0:T(8,128)} %get-tuple-element.240, f32[4,2,512]{2,1,0:T(2,128)} %copy-done.107, f32[4,2,512]{2,1,0:T(2,128)} %copy-done.109, pred[512,1024]{0,1:T(8,128)(4,1)} %fusion.77), kind=kOutput, calls=%fused_computation.191 | convolution fusion | flops 558366720 | bytes 18907136 | tf_op jit(solution)/shard_map/grqk,qgrd->kgd/dot_general | solution.py:498
  462.2 8.5 %collective-permute-done.31 = bf16[512,1024]{1,0:T(8,128)(2,1)S(1)} collective-permute-done((bf16[512,1024]{1,0:T(8,128)(2,1)S(1)}, bf16[512,1024]{1,0:T(8,128)(2,1)S(1)}, u32[]{:S(2)}, u32[]{:S(2)}) %collective-permute-start.31) | collective-permute-done | bytes 1048608 | tf_op jit(solution)/shard_map/ppermute | solution.py:245
  472.7 9.3 %collective-permute-done.38 = bf16[64,1536]{1,0:T(8,128)(2,1)S(1)} collective-permute-done((bf16[64,1536]{1,0:T(8,128)(2,1)S(1)}, bf16[64,1536]{1,0:T(8,128)(2,1)S(1)}, u32[]{:S(2)}, u32[]{:S(2)}) %collective-permute-start.38) | collective-permute-done | bytes 196640 | tf_op jit(solution)/shard_map/ppermute | solution.py:208
  (545 shorter events, 290.1 us)
Async XLA Ops:
  4.0 21.9 %collective-permute-start.1 = (bf16[64,1664]{1,0:T(8,128)(2,1)}, bf16[64,1664]{1,0:T(8,128)(2,1)}, u32[]{:S(2)}, u32[]{:S(2)}) collective-permute-start(bf16[64,1664]{1,0:T(8,128)(2,1)} %concatenate.121), channel_id=1, source_target_pairs={{0,8},{2,10},{8,16},{10,18},{16,24},{18,26},{24,28},{26,30},{28,20... | collective-permute-start | bytes 638984 | tf_op jit(solution)/shard_map/ppermute | solution.py:141
  7.0 20.9 %collective-permute-start.2 = (bf16[64,1664]{1,0:T(8,128)(2,1)}, bf16[64,1664]{1,0:T(8,128)(2,1)}, u32[]{:S(2)}, u32[]{:S(2)}) collective-permute-start(bf16[64,1664]{1,0:T(8,128)(2,1)} %concatenate.121), channel_id=1, source_target_pairs={{8,0},{10,2},{16,8},{18,10},{24,16},{26,18},{28,24},{30,26},{20,28... | collective-permute-start | bytes 638984 | tf_op jit(solution)/shard_map/ppermute | solution.py:144
  7.0 42.6 %collective-permute-start = (bf16[512,1024]{1,0:T(8,128)(2,1)}, bf16[512,1024]{1,0:T(8,128)(2,1)}, u32[]{:S(2)}, u32[]{:S(2)}) collective-permute-start(bf16[512,1024]{1,0:T(8,128)(2,1)} %param.26), channel_id=1, source_target_pairs={{1,0},{0,1},{3,2},{2,3},{5,4},{4,5},{7,6},{6,7},{9,8},{8,9},{11,10... | collective-permute-start | bytes 3145736 | tf_op jit(solution)/shard_map/ppermute | solution.py:245
  12.7 181.7 %collective-permute-start.22 = (bf16[512,1024]{1,0:T(8,128)(2,1)}, bf16[512,1024]{1,0:T(8,128)(2,1)}, u32[]{:S(2)}, u32[]{:S(2)}) collective-permute-start(bf16[512,1024]{1,0:T(8,128)(2,1)} %broadcast_select_fusion), channel_id=1, source_target_pairs={{1,0},{0,1},{3,2},{2,3},{5,4},{4,5},{7,6},{6,7},{9,8},{8,9},{11,10... | collective-permute-start | bytes 3145736 | tf_op jit(solution)/shard_map/ppermute | solution.py:245
  56.7 22.3 %collective-permute-start.10 = (bf16[64,6912]{1,0:T(8,128)(2,1)}, bf16[64,6912]{1,0:T(8,128)(2,1)}, u32[]{:S(2)}, u32[]{:S(2)}) collective-permute-start(bf16[64,6912]{1,0:T(8,128)(2,1)} %pad_maximum_fusion.11), channel_id=1, source_target_pairs={{0,8},{2,10},{8,16},{10,18},{16,24},{18,26},{24,28},{26,30},{28,20... | collective-permute-start | bytes 2654216 | tf_op jit(solution)/shard_map/ppermute | solution.py:141
  58.4 22.3 %collective-permute-start.11 = (bf16[64,6912]{1,0:T(8,128)(2,1)}, bf16[64,6912]{1,0:T(8,128)(2,1)}, u32[]{:S(2)}, u32[]{:S(2)}) collective-permute-start(bf16[64,6912]{1,0:T(8,128)(2,1)} %pad_maximum_fusion.11), channel_id=1, source_target_pairs={{8,0},{10,2},{16,8},{18,10},{24,16},{26,18},{28,24},{30,26},{20,28... | collective-permute-start | bytes 2654216 | tf_op jit(solution)/shard_map/ppermute | solution.py:144
  81.6 42.8 %collective-permute-start.12 = (bf16[64,6912]{1,0:T(8,128)(2,1)}, bf16[64,6912]{1,0:T(8,128)(2,1)}, u32[]{:S(2)}, u32[]{:S(2)}) collective-permute-start(bf16[64,6912]{1,0:T(8,128)(2,1)} %collective-permute-done.10), channel_id=1, source_target_pairs={{0,8},{2,10},{8,16},{10,18},{16,24},{18,26},{24,28},{26,30},{28,20... | collective-permute-start | bytes 2654216 | tf_op jit(solution)/shard_map/ppermute | solution.py:141
  83.1 41.2 %collective-permute-start.13 = (bf16[64,6912]{1,0:T(8,128)(2,1)}, bf16[64,6912]{1,0:T(8,128)(2,1)}, u32[]{:S(2)}, u32[]{:S(2)}) collective-permute-start(bf16[64,6912]{1,0:T(8,128)(2,1)} %collective-permute-done.11), channel_id=1, source_target_pairs={{8,0},{10,2},{16,8},{18,10},{24,16},{26,18},{28,24},{30,26},{20,28... | collective-permute-start | bytes 2654216 | tf_op jit(solution)/shard_map/ppermute | solution.py:144
  124.4 20.6 %collective-permute-start.14 = (bf16[64,6912]{1,0:T(8,128)(2,1)}, bf16[64,6912]{1,0:T(8,128)(2,1)S(1)}, u32[]{:S(2)}, u32[]{:S(2)}) collective-permute-start(bf16[64,6912]{1,0:T(8,128)(2,1)} %collective-permute-done.12), channel_id=1, source_target_pairs={{0,8},{2,10},{8,16},{10,18},{16,24},{18,26},{24,28},{26,30},{28,20... | collective-permute-start | bytes 2654216 | tf_op jit(solution)/shard_map/ppermute | solution.py:141
  126.0 20.8 %collective-permute-start.15 = (bf16[64,6912]{1,0:T(8,128)(2,1)}, bf16[64,6912]{1,0:T(8,128)(2,1)S(1)}, u32[]{:S(2)}, u32[]{:S(2)}) collective-permute-start(bf16[64,6912]{1,0:T(8,128)(2,1)} %collective-permute-done.13), channel_id=1, source_target_pairs={{8,0},{10,2},{16,8},{18,10},{24,16},{26,18},{28,24},{30,26},{20,28... | collective-permute-start | bytes 2654216 | tf_op jit(solution)/shard_map/ppermute | solution.py:144
  131.2 42.1 %collective-permute-start.17 = (bf16[5,64,6912]{2,1,0:T(8,128)(2,1)}, bf16[5,64,6912]{2,1,0:T(8,128)(2,1)S(1)}, u32[]{:S(2)}, u32[]{:S(2)}) collective-permute-start(bf16[5,64,6912]{2,1,0:T(8,128)(2,1)} %bitcast_dynamic-update-slice_fusion.3), channel_id=1, source_target_pairs={{0,2},{2,0},{4,6},{6,4},{8,10},{10,8},{12,14},{14,12},{16,18},{18,... | collective-permute-start | bytes 13271048 | tf_op jit(solution)/shard_map/ppermute | solution.py:158
  147.7 22.8 %collective-permute-start.16 = (bf16[512,1024]{1,0:T(8,128)(2,1)S(1)}, bf16[512,1024]{1,0:T(8,128)(2,1)S(1)}, u32[]{:S(2)}, u32[]{:S(2)}) collective-permute-start(bf16[512,1024]{1,0:T(8,128)(2,1)S(1)} %convolution_convert_fusion.4), channel_id=1, source_target_pairs={{1,0},{0,1},{3,2},{2,3},{5,4},{4,5},{7,6},{6,7},{9,8},{8,9},{11,10... | collective-permute-start | bytes 3145736 | tf_op jit(solution)/shard_map/ppermute | solution.py:245
  171.7 28.0 %collective-permute-start.20 = (bf16[512,1024]{1,0:T(8,128)(2,1)S(1)}, bf16[512,1024]{1,0:T(8,128)(2,1)S(1)}, u32[]{:S(2)}, u32[]{:S(2)}) collective-permute-start(bf16[512,1024]{1,0:T(8,128)(2,1)S(1)} %multiply_convert_fusion.6), channel_id=1, source_target_pairs={{1,0},{0,1},{3,2},{2,3},{5,4},{4,5},{7,6},{6,7},{9,8},{8,9},{11,10... | collective-permute-start | bytes 3145736 | tf_op jit(solution)/shard_map/ppermute | solution.py:245
  221.6 78.7 %collective-permute-start.21 = (bf16[512,1024]{1,0:T(8,128)(2,1)S(1)}, bf16[512,1024]{1,0:T(8,128)(2,1)S(1)}, u32[]{:S(2)}, u32[]{:S(2)}) collective-permute-start(bf16[512,1024]{1,0:T(8,128)(2,1)S(1)} %fusion.101), channel_id=1, source_target_pairs={{1,0},{0,1},{3,2},{2,3},{5,4},{4,5},{7,6},{6,7},{9,8},{8,9},{11,10... | collective-permute-start | bytes 3145736 | tf_op jit(solution)/shard_map/ppermute | solution.py:245
  255.9 80.4 %collective-permute-start.24 = (bf16[8,64,6912]{2,1,0:T(8,128)(2,1)}, bf16[8,64,6912]{2,1,0:T(8,128)(2,1)}, u32[]{:S(2)}, u32[]{:S(2)}) collective-permute-start(bf16[8,64,6912]{2,1,0:T(8,128)(2,1)} %pad_maximum_fusion), channel_id=1, source_target_pairs={{0,2},{2,0},{4,6},{6,4},{8,10},{10,8},{12,14},{14,12},{16,18},{18,... | collective-permute-start | bytes 21233672 | tf_op jit(solution)/shard_map/ppermute | solution.py:176
  265.6 25.5 %collective-permute-start.23 = (bf16[512,1024]{1,0:T(8,128)(2,1)S(1)}, bf16[512,1024]{1,0:T(8,128)(2,1)S(1)}, u32[]{:S(2)}, u32[]{:S(2)}) collective-permute-start(bf16[512,1024]{1,0:T(8,128)(2,1)S(1)} %add_convert_fusion.1), channel_id=1, source_target_pairs={{1,0},{0,1},{3,2},{2,3},{5,4},{4,5},{7,6},{6,7},{9,8},{8,9},{11,10... | collective-permute-start | bytes 3145736 | tf_op jit(solution)/shard_map/ppermute | solution.py:245
  298.0 24.7 %collective-permute-start.25 = (bf16[512,1024]{1,0:T(8,128)(2,1)S(1)}, bf16[512,1024]{1,0:T(8,128)(2,1)S(1)}, u32[]{:S(2)}, u32[]{:S(2)}) collective-permute-start(bf16[512,1024]{1,0:T(8,128)(2,1)S(1)} %fusion.226), channel_id=1, source_target_pairs={{1,0},{0,1},{3,2},{2,3},{5,4},{4,5},{7,6},{6,7},{9,8},{8,9},{11,10... | collective-permute-start | bytes 3145736 | tf_op jit(solution)/shard_map/ppermute | solution.py:245
  384.8 35.8 %collective-permute-start.30 = (bf16[64,6912]{1,0:T(8,128)(2,1)}, bf16[64,6912]{1,0:T(8,128)(2,1)}, u32[]{:S(2)}, u32[]{:S(2)}) collective-permute-start(bf16[64,6912]{1,0:T(8,128)(2,1)} %get-tuple-element.117), channel_id=1, source_target_pairs={{8,0},{10,2},{16,8},{18,10},{24,16},{26,18},{28,24},{30,26},{20,28... | collective-permute-start | bytes 2654216 | tf_op jit(solution)/shard_map/ppermute | solution.py:210
  385.3 35.3 %collective-permute-start.29 = (bf16[64,6912]{1,0:T(8,128)(2,1)}, bf16[64,6912]{1,0:T(8,128)(2,1)}, u32[]{:S(2)}, u32[]{:S(2)}) collective-permute-start(bf16[64,6912]{1,0:T(8,128)(2,1)} %get-tuple-element.116), channel_id=1, source_target_pairs={{0,8},{2,10},{8,16},{10,18},{16,24},{18,26},{24,28},{26,30},{28,20... | collective-permute-start | bytes 2654216 | tf_op jit(solution)/shard_map/ppermute | solution.py:208
  438.2 21.2 %collective-permute-start.37 = (bf16[8,64,1536]{2,1,0:T(8,128)(2,1)}, bf16[8,64,1536]{2,1,0:T(8,128)(2,1)}, u32[]{:S(2)}, u32[]{:S(2)}) collective-permute-start(bf16[8,64,1536]{2,1,0:T(8,128)(2,1)} %pad_maximum_fusion.5), channel_id=1, source_target_pairs={{0,2},{2,0},{4,6},{6,4},{8,10},{10,8},{12,14},{14,12},{16,18},{18,... | collective-permute-start | bytes 4718600 | tf_op jit(solution)/shard_map/ppermute | solution.py:176
  445.4 25.4 %collective-permute-start.31 = (bf16[512,1024]{1,0:T(8,128)(2,1)S(1)}, bf16[512,1024]{1,0:T(8,128)(2,1)S(1)}, u32[]{:S(2)}, u32[]{:S(2)}) collective-permute-start(bf16[512,1024]{1,0:T(8,128)(2,1)S(1)} %add_convert_fusion), channel_id=1, source_target_pairs={{1,0},{0,1},{3,2},{2,3},{5,4},{4,5},{7,6},{6,7},{9,8},{8,9},{11,10... | collective-permute-start | bytes 3145736 | tf_op jit(solution)/shard_map/ppermute | solution.py:245
  457.3 34.0 %collective-permute-start.51 = (bf16[64,6912]{1,0:T(8,128)(2,1)S(1)}, bf16[64,6912]{1,0:T(8,128)(2,1)S(1)}, u32[]{:S(2)}, u32[]{:S(2)}) collective-permute-start(bf16[64,6912]{1,0:T(8,128)(2,1)S(1)} %copy-done.68), channel_id=1, source_target_pairs={{8,0},{10,2},{16,8},{18,10},{24,16},{26,18},{28,24},{30,26},{20,28... | collective-permute-start | bytes 2654216 | tf_op jit(solution)/shard_map/ppermute | solution.py:210
  458.0 33.4 %collective-permute-start.50 = (bf16[64,6912]{1,0:T(8,128)(2,1)S(1)}, bf16[64,6912]{1,0:T(8,128)(2,1)S(1)}, u32[]{:S(2)}, u32[]{:S(2)}) collective-permute-start(bf16[64,6912]{1,0:T(8,128)(2,1)S(1)} %copy-done.67), channel_id=1, source_target_pairs={{0,8},{2,10},{8,16},{10,18},{16,24},{18,26},{24,28},{26,30},{28,20... | collective-permute-start | bytes 2654216 | tf_op jit(solution)/shard_map/ppermute | solution.py:208
  460.5 21.4 %collective-permute-start.38 = (bf16[64,1536]{1,0:T(8,128)(2,1)S(1)}, bf16[64,1536]{1,0:T(8,128)(2,1)S(1)}, u32[]{:S(2)}, u32[]{:S(2)}) collective-permute-start(bf16[64,1536]{1,0:T(8,128)(2,1)S(1)} %fusion.177), channel_id=1, source_target_pairs={{0,8},{2,10},{8,16},{10,18},{16,24},{18,26},{24,28},{26,30},{28,20... | collective-permute-start | bytes 589832 | tf_op jit(solution)/shard_map/ppermute | solution.py:208
  (161 other events, 2048.5 us)

commit v3 on v2

--- a/solution.py
+++ b/solution.py
@@ -394,6 +394,7 @@
         )
         kept_stats.append((row_peak, row_total))
         outputs[-1] = ffn_ring.advance(outputs[-1])
+        query_grouped, outputs[-1] = tie(query_grouped, outputs[-1])
     heads_low = (
         jnp.concatenate(outputs, axis=0)
         .reshape(group_rows, query_heads * head_dim)
@@ -417,18 +418,26 @@
                 grad_hidden * up_proj * sigmoid_gate * (1.0 + gate * (1.0 - sigmoid_gate))
             ).astype(jnp.bfloat16)
         )
-    grad_ffn_in = scatter_parts(
-        lambda k: contract_cols(grad_gates[k], wg_all) + contract_cols(grad_ups[k], wu_all)
-    )
+    ffn_cat = jnp.concatenate(ffn_parts, axis=0)
+    grad_cat = jnp.concatenate(grad_parts, axis=0)
+
+    def ffn_in_part(k):
+        return contract_cols(grad_gates[k], wg_all) + contract_cols(grad_ups[k], wu_all)
+
+    sends = [ffn_in_part(k).astype(jnp.bfloat16) for k in range(1, len(ffn_parts))]
+    ffn_cat, *sends = tie(ffn_cat, *sends)
+    grad_ffn_in = ffn_in_part(0)
+    for k, part in enumerate(sends):
+        grad_ffn_in = grad_ffn_in + shifted(part, -k - 1).astype(jnp.float32)
     back_mixed, ffn_gain_part = norm_back(
         mixed, ffn_inv, ffn_gain_all.astype(jnp.float32), grad_ffn_in
     )
     grad_mixed = grad_out.astype(jnp.float32) + back_mixed
-    mixed_parts = gather_parts(grad_mixed.astype(jnp.bfloat16))
-    result = mixed + scatter_parts(lambda k: contract_cols(hiddens[k], wdt_all))
+    mixed_low, grad_cat = tie(grad_mixed.astype(jnp.bfloat16), grad_cat)
+    mixed_parts = gather_parts(mixed_low)
+    mixed_parts[-1], *late = tie(mixed_parts[-1], *hiddens)
+    result = mixed + scatter_parts(lambda k: contract_cols(late[k], wdt_all))
     output = result.astype(jnp.bfloat16)
-    ffn_cat = jnp.concatenate(ffn_parts, axis=0)
-    grad_cat = jnp.concatenate(grad_parts, axis=0)
     ffn_sum_ring = Steps(
         ring_scatter(
             [
@@ -517,14 +526,20 @@
     grad_wq = contract_rows(attn_rows, grad_query_low)
     grad_wk = contract_rows(attn_rows, grad_key_low)
     grad_wv = contract_rows(attn_rows, grad_value_low)
-    grad_attn_in = scatter_parts(
-        lambda k: contract_cols(part_of(grad_query_low, k), wq_all)
+    attn_in_parts = [
+        contract_cols(part_of(grad_query_low, k), wq_all)
         + contract_cols(part_of(grad_key_low, k), wk_all)
         + contract_cols(part_of(grad_value_low, k), wv_all)
-    )
-    back_tokens, attn_gain_part = norm_back(
+        for k in range(len(token_parts))
+    ]
+    grad_attn_in = scatter_parts(lambda k: attn_in_parts[k])
+    back_tokens, _ = norm_back(
         tokens_wide, attn_inv, attn_gain_all.astype(jnp.float32), grad_attn_in
     )
+    attn_gain_sum = 0.0
+    for part, rows in zip(attn_in_parts, token_parts):
+        normed = rows_normalize(rows.astype(jnp.float32), 1.0)[0]
+        attn_gain_sum = attn_gain_sum + jnp.sum(part * normed, axis=0)
     input_grad = grad_mixed + back_tokens
     ffn_sum = ffn_sum_ring.finish()
     ffn_sums = (ffn_sum[:, :fw], ffn_sum[:, fw : 2 * fw], ffn_sum[:, 2 * fw :].T)
@@ -540,9 +555,10 @@
         attn_pack_sum[:, qw + 2 * kw :].T,
     )
     width = tokens.shape[1]
-    early = sum_everywhere(
+    summed = sum_everywhere(
         jnp.concatenate(
             [
+                attn_gain_sum,
                 jnp.sum(ffn_gain_part, axis=0),
                 jnp.sum(qgain_terms, axis=(0, 1)),
                 jnp.sum(kgain_terms, axis=(0, 1)),
@@ -550,10 +566,10 @@
         )
     )
     gain_sums = (
-        sum_everywhere(jnp.sum(attn_gain_part, axis=0)),
-        early[:width],
-        early[width : width + head_dim],
-        early[width + head_dim :],
+        summed[:width],
+        summed[width : 2 * width],
+        summed[2 * width : 2 * width + head_dim],
+        summed[2 * width + head_dim :],
     )
     gain_shard = attn_gain.shape[0]
     gain_start = lax.axis_index("dp") * gain_shard

time: 531 us -> 540 us (1.017)
  starting transfers between devices: 56 us -> 45.7 us
  other arithmetic: 65.4 us -> 75.1 us
  waiting for transfers between devices: 124 us -> 130 us
    ppermute x8, waiting for transfers between devices: 41.6 us -> 77.7 us  [shifted(): lax.ppermute(values, 'tensor', [((i + shift) % size, i) for i in range(si...]
    ppermute x7, waiting for transfers between devices: 19.8 us -> 1.16 us  [ring_gather(): from_right = lax.ppermute(from_right, 'dp', left)]
    dot_general x2 -> x4, matrix products: 8.75 us -> 18.5 us  [per_device(): jnp.einsum('qgrd,kgd->grqk', query_grouped[low_row:high_row], key_low[:hi...]
    sub x2, matrix products: 36.5 us -> 27.6 us  [per_device(): grad_scores = (probs_wide * (grad_probs - inner_sum)).astype(jnp.bfloat16)]
    ppermute x7, starting transfers between devices: 13.6 us -> 4.99 us  [ring_gather(): from_left = lax.ppermute(from_left, 'dp', right)]
    ppermute x7, starting transfers between devices: 2.49 us -> 9.92 us  [ring_gather(): from_right = lax.ppermute(from_right, 'dp', left)]
    dot_general x2, matrix products: 16 us -> 8.63 us  [per_device(): gate = jnp.dot(ffn_rows, wg_all, preferred_element_type=jnp.float32)]
    ppermute x7, waiting for transfers between devices: 24.4 us -> 17.9 us  [ring_gather(): from_left = lax.ppermute(from_left, 'dp', right)]
  transfers between devices with their start and end apart: 52 -> 47, of which waited for: 25 -> 20; matrix products, arithmetic and copies ran while one was open for 54% -> 53% of each run, Pallas kernels for 0% -> 0%
where the time goes in v3:
time: 540 us; the launch traced here: 533 us
  matrix products  197 us (36%)
  waiting for transfers between devices  130 us (24%)
  local copies, waits for them, and re-layouts  82.7 us (15%)
  other arithmetic  75.1 us (14%)
  starting transfers between devices  45.7 us (8%)
    ppermute x8, waiting for transfers between devices, shifted(): lax.ppermute(values, 'tensor', [((i + shift) % size, i) for i in range(si...  77.7 us
    dot_general x14, matrix products, contract_cols(): lax.dot_general(left, right, (((1,), (1,)), ((), ())), preferred_element_...  46.1 us
    sub x2, matrix products, per_device(): grad_scores = (probs_wide * (grad_probs - inner_sum)).astype(jnp.bfloat16)  27.6 us
    unnamed x300, local copies, waits for them, and re-layouts  26.9 us
    dot_general x7, matrix products, contract_rows(): lax.dot_general(left, right, (((0,), (0,)), ((), ())), preferred_element_...  25.8 us
    dynamic_update_slice x32, local copies, waits for them, and re-layouts, put(): lax.dynamic_update_slice(whole, value[None, None], (ring_chip(pos, chips)...  21.3 us
    convert_element_type x10, other arithmetic, ring_scatter(): sends.append(part.astype(jnp.bfloat16))  19 us
    dot_general x4, matrix products, per_device(): jnp.einsum('qgrd,kgd->grqk', query_grouped[low_row:high_row], key_low[:hi...  18.5 us
  transfers between devices with their start and end apart: 47, of which 20 were waited for; matrix products, arithmetic and copies ran while one was open for 53% of the time, Pallas kernels for 0%

profile of v3, /device:TPU:0, one launch (start us, length us, event | category | flops | bytes accessed | tf_op | source)
XLA Modules:
  0.0 533.2 jit_solution(3867561172960995693)
XLA Ops:
  31.8 6.8 %collective-permute-done.6 = bf16[64,1664]{1,0:T(8,128)(2,1)S(1)} collective-permute-done((bf16[64,1664]{1,0:T(8,128)(2,1)S(1)}, bf16[64,1664]{1,0:T(8,128)(2,1)S(1)}, u32[]{:S(2)}, u32[]{:S(2)}) %collective-permute-start.6) | collective-permute-done | bytes 213024 | tf_op jit(solution)/shard_map/ppermute | solution.py:141
  39.2 6.1 %collective-permute-done.8 = bf16[64,1664]{1,0:T(8,128)(2,1)S(1)} collective-permute-done((bf16[64,1664]{1,0:T(8,128)(2,1)S(1)}, bf16[64,1664]{1,0:T(8,128)(2,1)S(1)}, u32[]{:S(2)}, u32[]{:S(2)}) %collective-permute-start.8) | collective-permute-done | bytes 213024 | tf_op jit(solution)/shard_map/ppermute | solution.py:141
  48.5 9.8 %collective-permute-done = bf16[512,1024]{1,0:T(8,128)(2,1)} collective-permute-done((bf16[512,1024]{1,0:T(8,128)(2,1)}, bf16[512,1024]{1,0:T(8,128)(2,1)}, u32[]{:S(2)}, u32[]{:S(2)}) %collective-permute-start) | collective-permute-done | bytes 1048608 | tf_op jit(solution)/shard_map/ppermute | solution.py:245
  73.7 6.4 %broadcast_in_dim.212 = bf16[8,2,64,6912]{3,2,1,0:T(8,128)(2,1)} broadcast(bf16[]{:T(256)} %constant.446.clone.1), dimensions={} | broadcast | bytes 14155778 | tf_op jit(solution)/shard_map/broadcast_in_dim | solution.py:128
  114.2 7.3 %fusion.8 = (f32[4,2,512]{2,1,0:T(2,128)S(1)}, f32[4,1024,512,2]{2,1,3,0:T(8,128)}) fusion(pred[512,1024]{0,1:T(8,128)(4,1)S(1)} %copy-done.49, bf16[1024,4,2,64]{0,3,2,1:T(8,128)(2,1)S(1)} %bitcast.597, bf16[1024,4,32]{0,2,1:T(8,128)(2,1)S(1)} %get-tuple-element.207, bf16[1024,4,32]{0,2,1:T(8,128)(2,1)S(1)} %get-tuple-element.208), kind=kOutput, calls=%fused_computation.14 | convolution fusion | flops 550498304 | bytes 18366464 | tf_op jit(solution)/shard_map/qgrd,kgd->grqk/dot_general | solution.py:374
  121.5 9.2 %fusion.7 = f32[4,2,512]{2,1,0:T(2,128)S(1)} fusion(f32[4,1024,512,2]{2,1,3,0:T(8,128)} %get-tuple-element.267, f32[4,2,512]{2,1,0:T(2,128)S(1)} %get-tuple-element.266, pred[512,1024]{0,1:T(8,128)(4,1)} %fusion.83), kind=kLoop, calls=%fused_computation.13 | loop fusion | flops 16773120 | bytes 17334272 | tf_op jit(solution)/shard_map/reduce_sum | solution.py:385
  130.8 8.4 %fusion.108 = bf16[512,4,2,64]{0,3,2,1:T(8,128)(2,1)S(1)} fusion(bf16[1024,4,64,1]{0,2,3,1:T(8,128)(2,1)} %bitcast.613, f32[4,1024,512,2]{2,1,3,0:T(8,128)} %get-tuple-element.267, f32[4,2,512]{2,1,0:T(2,128)S(1)} %fusion.7, f32[4,2,512]{2,1,0:T(2,128)S(1)} %get-tuple-element.266, pred[512,1024]{0,1:T(8,128)(4,1)} %fusion.83), kind=kOutput, calls=%fused_computation.185 | convolution fusion | flops 557842432 | bytes 18382848 | tf_op jit(solution)/shard_map/grqk,kgd->qgrd/dot_general | solution.py:388
  143.6 22.3 %collective-permute-done.16 = bf16[512,1024]{1,0:T(8,128)(2,1)S(1)} collective-permute-done((bf16[512,1024]{1,0:T(8,128)(2,1)S(1)}, bf16[512,1024]{1,0:T(8,128)(2,1)S(1)}, u32[]{:S(2)}, u32[]{:S(2)}) %collective-permute-start.16) | collective-permute-done | bytes 1048608 | tf_op jit(solution)/shard_map/ppermute | solution.py:245
  173.0 20.2 %collective-permute-done.20 = bf16[512,1024]{1,0:T(8,128)(2,1)S(1)} collective-permute-done((bf16[512,1024]{1,0:T(8,128)(2,1)S(1)}, bf16[512,1024]{1,0:T(8,128)(2,1)S(1)}, u32[]{:S(2)}, u32[]{:S(2)}) %collective-permute-start.20) | collective-permute-done | bytes 1048608 | tf_op jit(solution)/shard_map/ppermute | solution.py:245
  211.5 6.0 %fusion.56 = f32[512,2304]{1,0:T(8,128)} fusion(bf16[512,1024]{1,0:T(8,128)(2,1)} %collective-permute-done.21, bf16[1024,6912]{1,0:T(8,128)(2,1)S(1)} %bitcast.582), kind=kOutput, calls=%fused_computation.96 | convolution fusion | flops 2415919104 | bytes 10485760 | tf_op jit(solution)/shard_map/dot_general | solution.py:412
  221.8 8.7 %multiply_convert_fusion = (bf16[512,2304]{1,0:T(8,128)(2,1)}, bf16[512,2304]{1,0:T(8,128)(2,1)}, bf16[512,2304]{1,0:T(8,128)(2,1)}) fusion(f32[512,2304]{1,0:T(8,128)} %fusion.38, f32[512,2304]{1,0:T(8,128)} %fusion.56, bf16[512,1024]{1,0:T(8,128)(2,1)S(1)} %collective-permute-done.20, bf16[1024,6912]{1,0:T(8,128)(2,1)S(1)} %bitcast.584), kind=kOutput, calls=%fused_computation.51 | convolution fusion | flops 2434793472 | bytes 22282240 | tf_op jit(solution)/shard_map/dot_general | solution.py:411
  239.1 8.3 %multiply_convert_fusion.1 = (bf16[512,2304]{1,0:T(8,128)(2,1)}, bf16[512,2304]{1,0:T(8,128)(2,1)}, bf16[512,2304]{1,0:T(8,128)(2,1)}) fusion(f32[512,2304]{1,0:T(8,128)} %fusion.42, f32[512,2304]{1,0:T(8,128)S(1)} %fusion.58, bf16[512,1024]{1,0:T(8,128)(2,1)S(1)} %multiply_convert_fusion.6, bf16[1024,6912]{1,0:T(8,128)(2,1)S(1)} %bitcast.587), kind=kOutput, calls=%fused_computation.52 | convolution fusion | flops 2434793472 | bytes 22282240 | tf_op jit(solution)/shard_map/dot_general | solution.py:411
  251.9 5.8 %convolution_convert_fusion.2 = bf16[1024,2304]{1,0:T(8,128)(2,1)S(1)} fusion(bf16[1024,1024]{1,0:T(8,128)(2,1)S(1)} %pad_maximum_fusion.2, bf16[512,2304]{1,0:T(8,128)(2,1)S(1)} %copy-done.137, bf16[512,2304]{1,0:T(8,128)(2,1)S(1)} %copy-done.139), kind=kOutput, calls=%fused_computation.35 | convolution fusion | flops 4843634688 | bytes 11534336 | tf_op jit(solution)/shard_map/dot_general | solution.py:82
  257.7 6.0 %fusion.48 = f32[512,1024]{1,0:T(8,128)S(1)} fusion(bf16[512,2304]{1,0:T(8,128)(2,1)} %get-tuple-element.157, bf16[1024,6912]{1,0:T(8,128)(2,1)S(1)} %bitcast.589), kind=kOutput, calls=%fused_computation.88 | convolution fusion | flops 2415919104 | bytes 9175040 | tf_op jit(solution)/shard_map/dot_general | solution.py:88
  266.1 5.8 %convolution_convert_fusion.1 = bf16[1024,2304]{1,0:T(8,128)(2,1)S(1)} fusion(bf16[1024,1024]{1,0:T(8,128)(2,1)S(1)} %pad_maximum_fusion.2, bf16[512,2304]{1,0:T(8,128)(2,1)S(1)} %copy-done.135, bf16[512,2304]{1,0:T(8,128)(2,1)S(1)} %copy-done.138), kind=kOutput, calls=%fused_computation.34 | convolution fusion | flops 4843634688 | bytes 11534336 | tf_op jit(solution)/shard_map/dot_general | solution.py:82
  278.1 5.6 %convolution_convert_fusion = bf16[1024,2304]{1,0:T(8,128)(2,1)S(1)} fusion(bf16[1024,1024]{1,0:T(8,128)(2,1)S(1)} %copy-done.51, bf16[512,2304]{1,0:T(8,128)(2,1)S(1)} %copy-done.134, bf16[512,2304]{1,0:T(8,128)(2,1)S(1)} %copy-done.132), kind=kOutput, calls=%fused_computation.33 | convolution fusion | flops 4843634688 | bytes 11534336 | tf_op jit(solution)/shard_map/dot_general | solution.py:82
  303.1 17.4 %collective-permute-done.23 = bf16[512,1024]{1,0:T(8,128)(2,1)S(1)} collective-permute-done((bf16[512,1024]{1,0:T(8,128)(2,1)}, bf16[512,1024]{1,0:T(8,128)(2,1)S(1)}, u32[]{:S(2)}, u32[]{:S(2)}) %collective-permute-start.23) | collective-permute-done | bytes 1048608 | tf_op jit(solution)/shard_map/ppermute | solution.py:245
  325.8 6.8 %fusion.105 = bf16[512,1024]{1,0:T(8,128)(2,1)} fusion(bf16[512,2304]{1,0:T(8,128)(2,1)} %get-tuple-element.127, bf16[1024,6912]{1,0:T(8,128)(2,1)} %bitcast.590), kind=kOutput, calls=%fused_computation.182 | convolution fusion | flops 2416443392 | bytes 8126464 | tf_op jit(solution)/shard_map/dot_general | solution.py:88
  346.9 9.8 %fusion.10 = bf16[4,2,512,512]{2,3,1,0:T(8,128)(2,1)} fusion(f32[4,2,512,512]{2,3,1,0:T(8,128)} %fusion.13, bf16[512,4,64,1]{0,2,3,1:T(8,128)(2,1)} %bitcast.615, bf16[512,4,2,64]{0,3,2,1:T(8,128)(2,1)S(1)} %bitcast.594), kind=kOutput, calls=%fused_computation.18 | convolution fusion | flops 545264128 | bytes 13369344 | tf_op jit(solution)/shard_map/sub | solution.py:486
  376.1 8.4 %collective-permute-done.27 = bf16[64,6912]{1,0:T(8,128)(2,1)S(1)} collective-permute-done((bf16[64,6912]{1,0:T(8,128)(2,1)S(1)}, bf16[64,6912]{1,0:T(8,128)(2,1)S(1)}, u32[]{:S(2)}, u32[]{:S(2)}) %collective-permute-start.27) | collective-permute-done | bytes 884768 | tf_op jit(solution)/shard_map/ppermute | solution.py:208
  396.2 5.7 %fusion.121 = bf16[1024,4,64]{0,2,1:T(8,128)(2,1)} fusion(bf16[512,4,2,64]{0,3,2,1:T(8,128)(2,1)S(1)} %bitcast.592, f32[4,2,512,1024]{2,3,1,0:T(8,128)S(1)} %fusion.6, f32[512,4,64]{0,2,1:T(8,128)} %fusion.126), kind=kOutput, calls=%fused_computation.200 | convolution fusion | flops 541589504 | bytes 18350080 | tf_op jit(solution)/shard_map/grqk,qgrd->kgd/dot_general | solution.py:507
  406.4 17.8 %fusion.3 = bf16[4,2,512,1024]{2,3,1,0:T(8,128)(2,1)} fusion(f32[4,2,512,1024]{2,3,1,0:T(8,128)} %copy-done, bf16[1024,4,64,1]{0,2,3,1:T(8,128)(2,1)S(1)} %bitcast.614, bf16[512,4,2,64]{0,3,2,1:T(8,128)(2,1)S(1)} %bitcast.593), kind=kOutput, calls=%fused_computation.5 | convolution fusion | flops 1090524160 | bytes 26214400 | tf_op jit(solution)/shard_map/sub | solution.py:486
  454.0 6.2 %add_convert_fusion = bf16[512,1024]{1,0:T(8,128)(2,1)} fusion(f32[512,1024]{1,0:T(8,128)S(1)} %get-tuple-element.269, bf16[512,1024]{1,0:T(8,128)(2,1)} %collective-permute-done.24, bf16[512,2304]{1,0:T(8,128)(2,1)S(1)} %copy-done.133, bf16[1024,6912]{1,0:T(8,128)(2,1)} %bitcast.591), kind=kOutput, calls=%fused_computation.142 | convolution fusion | flops 2418016256 | bytes 11272192 | tf_op jit(solution)/shard_map/dot_general | solution.py:88
  468.9 8.0 %collective-permute-done.31 = bf16[512,1024]{1,0:T(8,128)(2,1)} collective-permute-done((bf16[512,1024]{1,0:T(8,128)(2,1)}, bf16[512,1024]{1,0:T(8,128)(2,1)}, u32[]{:S(2)}, u32[]{:S(2)}) %collective-permute-start.31) | collective-permute-done | bytes 1048608 | tf_op jit(solution)/shard_map/ppermute | solution.py:245
  (566 shorter events, 306.9 us)
Async XLA Ops:
  10.9 34.5 %collective-permute-start.21 = (bf16[512,1024]{1,0:T(8,128)(2,1)}, bf16[512,1024]{1,0:T(8,128)(2,1)}, u32[]{:S(2)}, u32[]{:S(2)}) collective-permute-start(bf16[512,1024]{1,0:T(8,128)(2,1)} %broadcast_select_fusion), channel_id=1, source_target_pairs={{1,0},{0,1},{3,2},{2,3},{5,4},{4,5},{7,6},{6,7},{9,8},{8,9},{11,10... | collective-permute-start | bytes 3145736 | tf_op jit(solution)/shard_map/ppermute | solution.py:245
  12.9 45.5 %collective-permute-start = (bf16[512,1024]{1,0:T(8,128)(2,1)}, bf16[512,1024]{1,0:T(8,128)(2,1)}, u32[]{:S(2)}, u32[]{:S(2)}) collective-permute-start(bf16[512,1024]{1,0:T(8,128)(2,1)} %param.26), channel_id=1, source_target_pairs={{1,0},{0,1},{3,2},{2,3},{5,4},{4,5},{7,6},{6,7},{9,8},{8,9},{11,10... | collective-permute-start | bytes 3145736 | tf_op jit(solution)/shard_map/ppermute | solution.py:245
  29.6 31.3 %collective-permute-start.5 = (bf16[5,64,1664]{2,1,0:T(8,128)(2,1)S(1)}, bf16[5,64,1664]{2,1,0:T(8,128)(2,1)S(1)}, u32[]{:S(2)}, u32[]{:S(2)}) collective-permute-start(bf16[5,64,1664]{2,1,0:T(8,128)(2,1)S(1)} %bitcast_dynamic-update-slice_fusion.16), channel_id=1, source_target_pairs={{0,2},{2,0},{4,6},{6,4},{8,10},{10,8},{12,14},{14,12},{16,18},{18,... | collective-permute-start | bytes 3194888 | tf_op jit(solution)/shard_map/ppermute | solution.py:158
  61.4 24.7 %collective-permute-start.11 = (bf16[64,6912]{1,0:T(8,128)(2,1)}, bf16[64,6912]{1,0:T(8,128)(2,1)}, u32[]{:S(2)}, u32[]{:S(2)}) collective-permute-start(bf16[64,6912]{1,0:T(8,128)(2,1)} %pad_maximum_fusion.10), channel_id=1, source_target_pairs={{8,0},{10,2},{16,8},{18,10},{24,16},{26,18},{28,24},{30,26},{20,28... | collective-permute-start | bytes 2654216 | tf_op jit(solution)/shard_map/ppermute | solution.py:144
  63.1 23.0 %collective-permute-start.10 = (bf16[64,6912]{1,0:T(8,128)(2,1)}, bf16[64,6912]{1,0:T(8,128)(2,1)}, u32[]{:S(2)}, u32[]{:S(2)}) collective-permute-start(bf16[64,6912]{1,0:T(8,128)(2,1)} %pad_maximum_fusion.10), channel_id=1, source_target_pairs={{0,8},{2,10},{8,16},{10,18},{16,24},{18,26},{24,28},{26,30},{28,20... | collective-permute-start | bytes 2654216 | tf_op jit(solution)/shard_map/ppermute | solution.py:141
  107.3 31.9 %collective-permute-start.14 = (bf16[64,6912]{1,0:T(8,128)(2,1)}, bf16[64,6912]{1,0:T(8,128)(2,1)}, u32[]{:S(2)}, u32[]{:S(2)}) collective-permute-start(bf16[64,6912]{1,0:T(8,128)(2,1)} %collective-permute-done.12), channel_id=1, source_target_pairs={{0,8},{2,10},{8,16},{10,18},{16,24},{18,26},{24,28},{26,30},{28,20... | collective-permute-start | bytes 2654216 | tf_op jit(solution)/shard_map/ppermute | solution.py:141
  111.1 28.2 %collective-permute-start.15 = (bf16[64,6912]{1,0:T(8,128)(2,1)}, bf16[64,6912]{1,0:T(8,128)(2,1)}, u32[]{:S(2)}, u32[]{:S(2)}) collective-permute-start(bf16[64,6912]{1,0:T(8,128)(2,1)} %collective-permute-done.13), channel_id=1, source_target_pairs={{8,0},{10,2},{16,8},{18,10},{24,16},{26,18},{28,24},{30,26},{20,28... | collective-permute-start | bytes 2654216 | tf_op jit(solution)/shard_map/ppermute | solution.py:144
  114.2 79.2 %collective-permute-start.17 = (bf16[5,64,6912]{2,1,0:T(8,128)(2,1)}, bf16[5,64,6912]{2,1,0:T(8,128)(2,1)}, u32[]{:S(2)}, u32[]{:S(2)}) collective-permute-start(bf16[5,64,6912]{2,1,0:T(8,128)(2,1)} %bitcast_dynamic-update-slice_fusion.3), channel_id=1, source_target_pairs={{0,2},{2,0},{4,6},{6,4},{8,10},{10,8},{12,14},{14,12},{16,18},{18,... | collective-permute-start | bytes 13271048 | tf_op jit(solution)/shard_map/ppermute | solution.py:158
  140.2 25.6 %collective-permute-start.16 = (bf16[512,1024]{1,0:T(8,128)(2,1)S(1)}, bf16[512,1024]{1,0:T(8,128)(2,1)S(1)}, u32[]{:S(2)}, u32[]{:S(2)}) collective-permute-start(bf16[512,1024]{1,0:T(8,128)(2,1)S(1)} %convolution_convert_fusion.4), channel_id=1, source_target_pairs={{1,0},{0,1},{3,2},{2,3},{5,4},{4,5},{7,6},{6,7},{9,8},{8,9},{11,10... | collective-permute-start | bytes 3145736 | tf_op jit(solution)/shard_map/ppermute | solution.py:245
  143.1 28.1 %collective-permute-start.18 = (bf16[64,6912]{1,0:T(8,128)(2,1)}, bf16[64,6912]{1,0:T(8,128)(2,1)S(1)}, u32[]{:S(2)}, u32[]{:S(2)}) collective-permute-start(bf16[64,6912]{1,0:T(8,128)(2,1)} %collective-permute-done.15), channel_id=1, source_target_pairs={{8,0},{10,2},{16,8},{18,10},{24,16},{26,18},{28,24},{30,26},{20,28... | collective-permute-start | bytes 2654216 | tf_op jit(solution)/shard_map/ppermute | solution.py:144
  168.4 24.8 %collective-permute-start.20 = (bf16[512,1024]{1,0:T(8,128)(2,1)S(1)}, bf16[512,1024]{1,0:T(8,128)(2,1)S(1)}, u32[]{:S(2)}, u32[]{:S(2)}) collective-permute-start(bf16[512,1024]{1,0:T(8,128)(2,1)S(1)} %multiply_convert_fusion.6), channel_id=1, source_target_pairs={{1,0},{0,1},{3,2},{2,3},{5,4},{4,5},{7,6},{6,7},{9,8},{8,9},{11,10... | collective-permute-start | bytes 3145736 | tf_op jit(solution)/shard_map/ppermute | solution.py:245
  172.9 29.3 %collective-permute-start.19 = (bf16[3,64,6912]{2,1,0:T(8,128)(2,1)S(1)}, bf16[3,64,6912]{2,1,0:T(8,128)(2,1)S(1)}, u32[]{:S(2)}, u32[]{:S(2)}) collective-permute-start(bf16[3,64,6912]{2,1,0:T(8,128)(2,1)S(1)} %pad_maximum_fusion.1), channel_id=1, source_target_pairs={{0,2},{2,0},{4,6},{6,4},{8,10},{10,8},{12,14},{14,12},{16,18},{18,... | collective-permute-start | bytes 7962632 | tf_op jit(solution)/shard_map/ppermute | solution.py:158
  237.6 34.3 %collective-permute-start.22 = (bf16[512,1024]{1,0:T(8,128)(2,1)S(1)}, bf16[512,1024]{1,0:T(8,128)(2,1)S(1)}, u32[]{:S(2)}, u32[]{:S(2)}) collective-permute-start(bf16[512,1024]{1,0:T(8,128)(2,1)S(1)} %add_convert_fusion.1), channel_id=1, source_target_pairs={{1,0},{0,1},{3,2},{2,3},{5,4},{4,5},{7,6},{6,7},{9,8},{8,9},{11,10... | collective-permute-start | bytes 3145736 | tf_op jit(solution)/shard_map/ppermute | solution.py:245
  289.5 48.5 %collective-permute-start.25 = (bf16[8,64,6912]{2,1,0:T(8,128)(2,1)}, bf16[8,64,6912]{2,1,0:T(8,128)(2,1)}, u32[]{:S(2)}, u32[]{:S(2)}) collective-permute-start(bf16[8,64,6912]{2,1,0:T(8,128)(2,1)} %pad_maximum_fusion), channel_id=1, source_target_pairs={{0,2},{2,0},{4,6},{6,4},{8,10},{10,8},{12,14},{14,12},{16,18},{18,... | collective-permute-start | bytes 21233672 | tf_op jit(solution)/shard_map/ppermute | solution.py:176
  294.7 25.8 %collective-permute-start.23 = (bf16[512,1024]{1,0:T(8,128)(2,1)}, bf16[512,1024]{1,0:T(8,128)(2,1)S(1)}, u32[]{:S(2)}, u32[]{:S(2)}) collective-permute-start(bf16[512,1024]{1,0:T(8,128)(2,1)} %fusion.236), channel_id=1, source_target_pairs={{1,0},{0,1},{3,2},{2,3},{5,4},{4,5},{7,6},{6,7},{9,8},{8,9},{11,10... | collective-permute-start | bytes 3145736 | tf_op jit(solution)/shard_map/ppermute | solution.py:245
  332.6 121.4 %collective-permute-start.24 = (bf16[512,1024]{1,0:T(8,128)(2,1)}, bf16[512,1024]{1,0:T(8,128)(2,1)}, u32[]{:S(2)}, u32[]{:S(2)}) collective-permute-start(bf16[512,1024]{1,0:T(8,128)(2,1)} %fusion.105), channel_id=1, source_target_pairs={{1,0},{0,1},{3,2},{2,3},{5,4},{4,5},{7,6},{6,7},{9,8},{8,9},{11,10... | collective-permute-start | bytes 3145736 | tf_op jit(solution)/shard_map/ppermute | solution.py:245
  340.4 21.3 %collective-permute-start.26 = (bf16[64,6912]{1,0:T(8,128)(2,1)}, bf16[64,6912]{1,0:T(8,128)(2,1)}, u32[]{:S(2)}, u32[]{:S(2)}) collective-permute-start(bf16[64,6912]{1,0:T(8,128)(2,1)} %fusion.97), channel_id=1, source_target_pairs={{0,8},{2,10},{8,16},{10,18},{16,24},{18,26},{24,28},{26,30},{28,20... | collective-permute-start | bytes 2654216 | tf_op jit(solution)/shard_map/ppermute | solution.py:208
  364.4 20.1 %collective-permute-start.27 = (bf16[64,6912]{1,0:T(8,128)(2,1)S(1)}, bf16[64,6912]{1,0:T(8,128)(2,1)S(1)}, u32[]{:S(2)}, u32[]{:S(2)}) collective-permute-start(bf16[64,6912]{1,0:T(8,128)(2,1)S(1)} %get-tuple-element.135), channel_id=1, source_target_pairs={{0,8},{2,10},{8,16},{10,18},{16,24},{18,26},{24,28},{26,30},{28,20... | collective-permute-start | bytes 2654216 | tf_op jit(solution)/shard_map/ppermute | solution.py:208
  389.2 35.0 %collective-permute-start.29 = (bf16[64,6912]{1,0:T(8,128)(2,1)}, bf16[64,6912]{1,0:T(8,128)(2,1)}, u32[]{:S(2)}, u32[]{:S(2)}) collective-permute-start(bf16[64,6912]{1,0:T(8,128)(2,1)} %get-tuple-element.138), channel_id=1, source_target_pairs={{0,8},{2,10},{8,16},{10,18},{16,24},{18,26},{24,28},{26,30},{28,20... | collective-permute-start | bytes 2654216 | tf_op jit(solution)/shard_map/ppermute | solution.py:208
  390.8 33.4 %collective-permute-start.30 = (bf16[64,6912]{1,0:T(8,128)(2,1)}, bf16[64,6912]{1,0:T(8,128)(2,1)}, u32[]{:S(2)}, u32[]{:S(2)}) collective-permute-start(bf16[64,6912]{1,0:T(8,128)(2,1)} %get-tuple-element.139), channel_id=1, source_target_pairs={{8,0},{10,2},{16,8},{18,10},{24,16},{26,18},{28,24},{30,26},{20,28... | collective-permute-start | bytes 2654216 | tf_op jit(solution)/shard_map/ppermute | solution.py:210
  446.4 39.4 %collective-permute-start.37 = (bf16[8,64,1536]{2,1,0:T(8,128)(2,1)}, bf16[8,64,1536]{2,1,0:T(8,128)(2,1)}, u32[]{:S(2)}, u32[]{:S(2)}) collective-permute-start(bf16[8,64,1536]{2,1,0:T(8,128)(2,1)} %pad_maximum_fusion.6), channel_id=1, source_target_pairs={{0,2},{2,0},{4,6},{6,4},{8,10},{10,8},{12,14},{14,12},{16,18},{18,... | collective-permute-start | bytes 4718600 | tf_op jit(solution)/shard_map/ppermute | solution.py:176
  452.6 24.3 %collective-permute-start.31 = (bf16[512,1024]{1,0:T(8,128)(2,1)}, bf16[512,1024]{1,0:T(8,128)(2,1)}, u32[]{:S(2)}, u32[]{:S(2)}) collective-permute-start(bf16[512,1024]{1,0:T(8,128)(2,1)} %get-tuple-element.197), channel_id=1, source_target_pairs={{1,0},{0,1},{3,2},{2,3},{5,4},{4,5},{7,6},{6,7},{9,8},{8,9},{11,10... | collective-permute-start | bytes 3145736 | tf_op jit(solution)/shard_map/ppermute | solution.py:245
  462.2 26.4 %collective-permute-start.45 = (bf16[64,6912]{1,0:T(8,128)(2,1)}, bf16[64,6912]{1,0:T(8,128)(2,1)}, u32[]{:S(2)}, u32[]{:S(2)}) collective-permute-start(bf16[64,6912]{1,0:T(8,128)(2,1)} %get-tuple-element.141), channel_id=1, source_target_pairs={{0,8},{2,10},{8,16},{10,18},{16,24},{18,26},{24,28},{26,30},{28,20... | collective-permute-start | bytes 2654216 | tf_op jit(solution)/shard_map/ppermute | solution.py:208
  463.8 24.8 %collective-permute-start.46 = (bf16[64,6912]{1,0:T(8,128)(2,1)}, bf16[64,6912]{1,0:T(8,128)(2,1)}, u32[]{:S(2)}, u32[]{:S(2)}) collective-permute-start(bf16[64,6912]{1,0:T(8,128)(2,1)} %get-tuple-element.142), channel_id=1, source_target_pairs={{8,0},{10,2},{16,8},{18,10},{24,16},{26,18},{28,24},{30,26},{20,28... | collective-permute-start | bytes 2654216 | tf_op jit(solution)/shard_map/ppermute | solution.py:210
  (169 other events, 1787.3 us)
